TPU v7x, 128 devices: a whole 4x4x4 slice. The times are simulated.
128 devices in a mesh: rows: 16 (over y, z), cols: 8 (over x, core).
Axes of the slice: x: 4, y: 4, z: 4, core: 2. Of those that a mesh axis runs over, the one named last changes fastest.
Arguments:
- iterate: bfloat16 [65536, 128], P(('rows', 'cols')), may hold values from -6 to 6
- blocks: bfloat16 [16, 8, 384, 128, 128], P('rows', 'cols'), may hold values from -0.0546875 to 0.0546875
- block_row: int32 [16, 8, 384], P('rows', 'cols'), may hold values from 0 to 511, as said below
- block_col: int32 [16, 8, 384], P('rows', 'cols'), may hold values from 0 to 511, as said below
- block_count: int32 [16, 8], P('rows', 'cols'), may hold values from 96 to 384, as said below
Outputs:
- search: bfloat16 [65536, 128], P(('rows', 'cols'))
- projected: float32 [256, 256], replicated
Inputs may be any that keep to these rules, and one draw needn't show every extreme that they name: block_row[a, b, s] lies in row group a: block rows a * 4 * 8 to (a + 1) * 4 * 8 - 1. block_col[a, b, s] is a block column j with (j // 4) % 8 == b. `block_count`: at least two slots of every device are live; some device has all slots live.
All inputs are finite; a program needn't handle non-finite values.
Results may differ from a plain program's by a relative error of at most 0.0019.
Values may be sent and summed in bfloat16 or wider, within the bound.
A program may use at most 192 MiB of HBM per device.

v0:
```python
import jax
import jax.numpy as jnp
from jax import lax
from jax.sharding import PartitionSpec as P

BS = 128


def inner(left, right):
    return jnp.einsum("ik,il->kl", left, right, precision=lax.Precision.HIGHEST)


def mult(left, right):
    return jnp.dot(left, right, precision=lax.Precision.HIGHEST)


def shards(iterate, blocks, block_row, block_col, block_count):
    per_dev = iterate.shape[0] // BS
    col_groups = lax.axis_size("cols")
    group_blocks = per_dev * col_groups
    node_total = iterate.shape[0] * lax.axis_size("rows") * col_groups
    inverse = 1.0 / node_total
    values = blocks[0, 0]
    slot_count = values.shape[0]
    row_local = block_row[0, 0] - lax.axis_index("rows") * group_blocks
    col_global = block_col[0, 0]
    slab_index = col_global // group_blocks * per_dev + col_global % per_dev
    live_mask = jnp.arange(slot_count) < block_count[0, 0]
    row_hot = (
        (row_local[None, :] == jnp.arange(group_blocks)[:, None]) & live_mask[None, :]
    ).astype(jnp.float32)

    def apply_local(slab_rows):
        tile_set = slab_rows.reshape(-1, BS, slab_rows.shape[1])
        picked = tile_set[slab_index]
        product = jnp.einsum("nab,nbk->nak", values, picked, preferred_element_type=jnp.float32)
        summed = jnp.einsum("gn,nak->gak", row_hot, product, precision=lax.Precision.HIGHEST)
        return summed.reshape(group_blocks * BS, slab_rows.shape[1])

    row_weight = jnp.einsum(
        "gn,na->ga",
        row_hot,
        jnp.sum(values, axis=2, dtype=jnp.float32),
        precision=lax.Precision.HIGHEST,
    ).reshape(-1)
    iterate_slab = lax.all_gather(iterate, "rows", axis=0, tiled=True)
    adj_x, degree = (
        lax.psum_scatter(apply_local(iterate_slab), "cols", scatter_dimension=0, tiled=True),
        lax.psum_scatter(row_weight, "cols", scatter_dimension=0, tiled=True),
    )
    iter_f = iterate.astype(jnp.float32)
    lap_x = degree[:, None] * iter_f - adj_x
    theta_mat = inverse * lax.psum(inner(iter_f, lap_x), ("rows", "cols"))
    residual = lap_x - mult(iter_f, theta_mat)
    correlation = inverse * lax.psum(inner(iter_f, residual), ("rows", "cols"))
    cleaned = residual - mult(iter_f, correlation)
    gram_mat = inverse * lax.psum(inner(cleaned, cleaned), ("rows", "cols"))
    lower_factor = jnp.linalg.cholesky(gram_mat)
    search = lax.linalg.triangular_solve(
        lower_factor, cleaned, left_side=False, lower=True, transpose_a=True
    ).astype(jnp.bfloat16)
    search_f = search.astype(jnp.float32)
    search_slab = lax.all_gather(search, "rows", axis=0, tiled=True)
    adj_part = apply_local(search_slab)
    adj_q = lax.psum_scatter(
        adj_part.astype(jnp.bfloat16), "cols", scatter_dimension=0, tiled=True
    ).astype(jnp.float32)
    lap_q = degree[:, None] * search_f - adj_q
    cross_xq = inner(iter_f, lap_q)
    inner_qq = inner(search_f, lap_q)
    cross_qx = inner(search_f, lap_x)
    sum_xq, sum_qx, sum_qq = lax.psum((cross_xq, cross_qx, inner_qq), ("rows", "cols"))
    top_half = jnp.concatenate([theta_mat, inverse * sum_xq], axis=1)
    bottom_half = jnp.concatenate([inverse * sum_qx, inverse * sum_qq], axis=1)
    return (search, jnp.concatenate([top_half, bottom_half], axis=0))


def solution(mesh):
    placed = (
        P(("rows", "cols"), None),
        P("rows", "cols", None, None, None),
        P("rows", "cols", None),
        P("rows", "cols", None),
        P("rows", "cols"),
    )
    return jax.shard_map(
        shards,
        mesh=mesh,
        in_specs=placed,
        out_specs=(P(("rows", "cols"), None), P()),
        check_vma=False,
    )
```

profile of v0, /device:TPU:1, one launch (start us, length us, event | category | flops | bytes accessed | tf_op | source)
XLA Modules:
  0.0 929.9 jit_solution(83313555946719081)
XLA Ops:
  10.0 47.6 %all-gather.3.cloned.1.call-done = bf16[8192,128]{1,0:T(8,128)(2,1)} async-done(((bf16[512,128]{1,0:T(8,128)(2,1)}), bf16[8192,128]{1,0:T(8,128)(2,1)}) %all-gather.3.cloned.1.call-update) | async-done | bytes 2097168 | tf_op jit(solution)/shard_map/all_gather | solution.py:46
  57.6 13.0 %gather_fusion = bf16[384,128,128]{2,1,0:T(8,128)(2,1)} fusion(bf16[64,128,128]{2,1,0:T(8,128)(2,1)} %bitcast.85, s32[1024]{0:T(1024)S(1)} %pad_clamp_fusion), kind=kCustom, calls=%fused_computation | custom fusion | bytes 25167360 | tf_op jit(solution)/shard_map/gather | solution.py:35
  70.6 22.1 %fusion.4 = f32[384,128,128]{1,2,0:T(8,128)} fusion(bf16[384,128,128]{2,1,0:T(8,128)(2,1)} %gather_fusion, bf16[1,1,384,128,128]{4,3,2,1,0:T(8,128)(2,1)} %param.6), kind=kOutput, calls=%fused_computation.7 | convolution fusion | flops 1610612736 | bytes 50331648 | tf_op jit(solution)/shard_map/nab,nbk->nak/dot_general | solution.py:36
  92.7 24.8 %copy.45 = f32[384,128,128]{2,0,1:T(8,128)} copy(f32[384,128,128]{1,2,0:T(8,128)} %fusion.4) | data formatting | bytes 50331648 | tf_op jit(solution)/shard_map/nab,nbk->nak/dot_general | solution.py:36
  117.5 14.3 %fusion.24 = f32[32,128,128]{2,0,1:T(8,128)S(1)} fusion(f32[384,128,128]{2,0,1:T(8,128)} %copy.45, s32[384]{0:T(512)S(1)} %subtract_reduce_fusion, pred[384]{0:T(512)(128)(4,1)S(1)} %iota_compare_fusion.3), kind=kOutput, calls=%fused_computation.39 | convolution fusion | flops 2415943680 | bytes 27264896 | tf_op jit(solution)/shard_map/gn,nak->gak/dot_general | solution.py:37
  131.8 1.2 copy.46
  133.0 1.9 copy.47
  136.5 7.6 convert_reduce_fusion
  144.3 22.7 %all-reduce = f32[4096]{0:T(1024)S(1)} all-reduce(f32[4096]{0:T(1024)S(1)} %convolution_bitcast_fusion.5), channel_id=2, replica_groups=mesh['rows'=16,'cols'=8] {'cols'}, use_global_device_ids=true, to_apply=%region_1.2.clone | all-reduce | flops 4096 | bytes 32768
  167.0 1.9 convolution_bitcast_fusion.4
  169.0 142.1 %all-reduce.7.cloned.1.call-done = f32[128,128]{0,1:T(8,128)} async-done(((f32[128,128]{0,1:T(8,128)}), f32[128,128]{0,1:T(8,128)}) %all-reduce.7.cloned.1.call-update) | async-done | bytes 65552 | tf_op jit(solution)/shard_map/psum | solution.py:53
  311.0 1.3 fusion.11
  313.3 138.3 %all-reduce.9.cloned.1.call-done = f32[128,128]{0,1:T(8,128)} async-done(((f32[128,128]{0,1:T(8,128)}), f32[128,128]{0,1:T(8,128)}) %all-reduce.9.cloned.1.call-update) | async-done | bytes 65552 | tf_op jit(solution)/shard_map/psum | solution.py:55
  451.6 1.1 fusion.10
  452.7 1.0 fusion.36
  453.8 137.6 %all-reduce.11.cloned.1.call-done = f32[128,128]{0,1:T(8,128)} async-done(((f32[128,128]{0,1:T(8,128)}), f32[128,128]{0,1:T(8,128)}) %all-reduce.11.cloned.1.call-update) | async-done | bytes 65552 | tf_op jit(solution)/shard_map/psum | solution.py:57
  593.2 11.7 %cholesky.16 = f32[128,128]{1,0:T(8,128)S(1)} custom-call(f32[128,128]{1,0:T(8,128)S(1)} %fusion.18), custom_call_target="Cholesky" | custom-call | tf_op jit(solution)/shard_map/jit(cholesky)/cholesky | solution.py:58
  606.3 9.8 %custom-call.6 = f32[1,128,128]{1,2,0:T(8,128)S(1)} custom-call(f32[1,128,128]{2,1,0:T(8,128)S(1)} %fusion.16), custom_call_target="InvertDiagBlocksLowerTriangular" | custom-call | tf_op jit(solution)/shard_map/triangular_solve | solution.py:59
  616.1 1.1 convolution_convert_fusion.1
  617.4 43.7 %all-gather.5.cloned.1.call-done = bf16[8192,128]{0,1:T(8,128)(2,1)} async-done(((bf16[512,128]{0,1:T(8,128)(2,1)}), bf16[8192,128]{0,1:T(8,128)(2,1)}) %all-gather.5.cloned.1.call-update) | async-done | bytes 2097168 | tf_op jit(solution)/shard_map/all_gather | solution.py:63
  661.1 3.2 copy.65
  664.4 11.4 %gather_fusion.1 = bf16[384,128,128]{2,1,0:T(8,128)(2,1)} fusion(bf16[64,128,128]{2,1,0:T(8,128)(2,1)S(1)} %bitcast.84, s32[1024]{0:T(1024)S(1)} %pad_clamp_fusion), kind=kCustom, calls=%fused_computation.1 | custom fusion | bytes 25167360 | tf_op jit(solution)/shard_map/gather | solution.py:35
  675.7 22.1 %fusion.7 = f32[384,128,128]{1,2,0:T(8,128)} fusion(bf16[384,128,128]{2,1,0:T(8,128)(2,1)} %gather_fusion.1, bf16[1,1,384,128,128]{4,3,2,1,0:T(8,128)(2,1)} %param.6), kind=kOutput, calls=%fused_computation.8 | convolution fusion | flops 1610612736 | bytes 50331648 | tf_op jit(solution)/shard_map/nab,nbk->nak/dot_general | solution.py:36
  697.8 24.8 %copy.53 = f32[384,128,128]{2,0,1:T(8,128)} copy(f32[384,128,128]{1,2,0:T(8,128)} %fusion.7) | data formatting | bytes 50331648 | tf_op jit(solution)/shard_map/nab,nbk->nak/dot_general | solution.py:36
  722.6 14.3 %convolution_convert_fusion = bf16[32,128,128]{2,0,1:T(8,128)(2,1)S(1)} fusion(f32[384,128,128]{2,0,1:T(8,128)} %copy.53, s32[384]{0:T(512)S(1)} %subtract_reduce_fusion, pred[384]{0:T(512)(128)(4,1)S(1)} %iota_compare_fusion.3), kind=kOutput, calls=%fused_computation.9 | convolution fusion | flops 2416467968 | bytes 26216320 | tf_op jit(solution)/shard_map/gn,nak->gak/dot_general | solution.py:37
  736.9 1.5 copy.54
  738.5 1.4 copy.68
  740.0 0.9 fusion.15
  740.9 28.4 %reduce-scatter.5.cloned.1.call-done = bf16[512,128]{0,1:T(8,128)(2,1)} async-done(((bf16[4096,128]{0,1:T(8,128)(2,1)}), bf16[512,128]{0,1:T(8,128)(2,1)}) %reduce-scatter.5.cloned.1.call-update) | async-done | bytes 131088 | tf_op jit(solution)/shard_map/reduce_scatter | solution.py:65
  769.3 1.8 fusion.12
  771.1 1.8 convolution_bitcast_fusion.2
  773.7 146.8 %all-reduce.13.cloned.1.call-done = (f32[128,128]{0,1:T(8,128)}, f32[128,128]{0,1:T(8,128)}, f32[128,128]{0,1:T(8,128)}) async-done(((f32[128,128]{0,1:T(8,128)}, f32[128,128]{0,1:T(8,128)}, f32[128,128]{0,1:T(8,128)}), (f32[128,128]{0,1:T(8,128)}, f32[128,128]{0,1:T(8,128)}, f32[128,128]{0,1:T(8,128)})) %all-reduce.13.cloned.1.call-update) | async-done | bytes 196624 | tf_op jit(solution)/shard_map/psum | solution.py:72
  (48 shorter events, 11.3 us)
Async XLA Ops:
  7.2 50.5 %all-gather.3.cloned.1.call-start = ((), (), s32[]{:S(2)}) async-start(), calls=%async_computation.2 | async-start | bytes 2228224 | tf_op jit(solution)/shard_map/all_gather | solution.py:46
  7.9 159.2 %reduce-scatter.3.cloned.1.call-start = ((), (), s32[]{:S(2)}) async-start(), calls=%async_computation.3 | async-start | bytes 2359296 | tf_op jit(solution)/shard_map/reduce_scatter | solution.py:48
  117.4 17.7 %copy-start.1 = (bf16[512,128]{1,0:T(8,128)(2,1)S(1)}, bf16[512,128]{1,0:T(8,128)(2,1)}, u32[]{:S(2)}) copy-start(bf16[512,128]{1,0:T(8,128)(2,1)} %param.5) | copy-start | bytes 393220
  117.5 17.8 %copy-start.4 = (u32[128]{0:T(128)S(1)}, u32[128]{0:T(128)}, u32[]{:S(2)}) copy-start(u32[128]{0:T(128)} %constant.91) | copy-start | bytes 1540
  134.9 176.2 %all-reduce.7.cloned.1.call-start = ((), (), s32[]{:S(2)}) async-start(), calls=%async_computation.4 | async-start | bytes 131072 | tf_op jit(solution)/shard_map/psum | solution.py:53
  168.9 282.6 %all-reduce.9.cloned.1.call-start = ((), (), s32[]{:S(2)}) async-start(), calls=%async_computation.5 | async-start | bytes 131072 | tf_op jit(solution)/shard_map/psum | solution.py:55
  313.2 278.2 %all-reduce.11.cloned.1.call-start = ((), (), s32[]{:S(2)}) async-start(), calls=%async_computation.6 | async-start | bytes 131072 | tf_op jit(solution)/shard_map/psum | solution.py:57
  453.7 207.4 %all-gather.5.cloned.1.call-start = ((), (), s32[]{:S(2)}) async-start(), calls=%async_computation.7 | async-start | bytes 2228224 | tf_op jit(solution)/shard_map/all_gather | solution.py:63
  617.2 152.1 %reduce-scatter.5.cloned.1.call-start = ((), (), s32[]{:S(2)}) async-start(), calls=%async_computation.8 | async-start | bytes 1179648 | tf_op jit(solution)/shard_map/reduce_scatter | solution.py:65
  722.6 17.4 %copy-start = (bf16[512,128]{0,1:T(8,128)(2,1)S(1)}, bf16[512,128]{0,1:T(8,128)(2,1)}, u32[]{:S(2)}) copy-start(bf16[512,128]{0,1:T(8,128)(2,1)} %convolution_convert_fusion.1) | copy-start | bytes 393220
  722.6 17.4 %copy-start.2 = (f32[512,128]{0,1:T(8,128)S(1)}, f32[512,128]{0,1:T(8,128)}, u32[]{:S(2)}) copy-start(f32[512,128]{0,1:T(8,128)} %reduce-scatter.3.cloned.1.call-done) | copy-start | bytes 786436
  722.6 50.3 %copy-start.3 = (f32[128,128]{0,1:T(8,128)S(1)}, f32[128,128]{0,1:T(8,128)}, u32[]{:S(2)}) copy-start(f32[128,128]{0,1:T(8,128)} %all-reduce.7.cloned.1.call-done) | copy-start | bytes 196612
  739.9 180.6 %all-reduce.13.cloned.1.call-start = ((), (), s32[]{:S(2)}) async-start(), calls=%async_computation.9 | async-start | bytes 393216 | tf_op jit(solution)/shard_map/psum | solution.py:72
Sparse Core Ops, SparseCore 0:
  10.1 47.4 all-gather.2
  135.0 30.9 reduce-scatter.2
  171.3 139.6 all-reduce.6
  316.9 134.5 all-reduce.8
  456.7 134.6 all-reduce.10
  617.3 43.7 all-gather.4
  740.1 29.1 reduce-scatter.4
  775.7 144.7 all-reduce.12
where the time goes:
time: 931 us; the launch traced here: 930 us
  waiting for transfers between devices  685 us (74%)
  local copies, waits for them, and re-layouts  85.6 us (9%)
  matrix products  84.8 us (9%)
  other arithmetic  35.3 us (4%)
  blocking collectives  22.7 us (2%)
  between operations  15.6 us (2%)
    psum x1, waiting for transfers between devices, shards(): lax.psum((cross_xq, cross_qx, inner_qq), ('rows', 'cols'))  147 us
    psum x1, waiting for transfers between devices, shards(): theta_mat = inverse * lax.psum(inner(iter_f, lap_x), ('rows', 'cols'))  142 us
    psum x1, waiting for transfers between devices, shards(): correlation = inverse * lax.psum(inner(iter_f, residual), ('rows', 'cols'))  138 us
    psum x1, waiting for transfers between devices, shards(): gram_mat = inverse * lax.psum(inner(cleaned, cleaned), ('rows', 'cols'))  138 us
    dot_general x2, local copies, waits for them, and re-layouts, apply_local(): jnp.einsum('nab,nbk->nak', values, picked, preferred_element_type=jnp.flo...  49.5 us
    all_gather x1, waiting for transfers between devices, shards(): iterate_slab = lax.all_gather(iterate, 'rows', axis=0, tiled=True)  47.6 us
    dot_general x2, matrix products, apply_local(): jnp.einsum('nab,nbk->nak', values, picked, preferred_element_type=jnp.flo...  44.2 us
    all_gather x1, waiting for transfers between devices, shards(): search_slab = lax.all_gather(search, 'rows', axis=0, tiled=True)  43.7 us
  transfers between devices with their start and end apart: 8, of which 7 were waited for; matrix products, arithmetic and copies ran while one was open for 1% of the time, Pallas kernels for 0%

commit v1 on v0

v1 whole, which is shorter than its diff:
```python
import jax
import jax.numpy as jnp
from jax import lax
from jax.experimental import pallas as pl
from jax.experimental.pallas import tpu as pltpu
from jax.sharding import PartitionSpec as P

BS = 128
NY = 4
NZ = 4
NX = 4
NCOL = 8
GROUP = 32
SLOTS = 384
PAIRS = (SLOTS + GROUP) // 2
UNROLL = 16
DEG = 8
N_SEM = 112

F32 = jnp.float32
BF16 = jnp.bfloat16
HI = lax.Precision.HIGHEST


def nt(a, b, precision=None):
    return lax.dot_general(a, b, (((1,), (1,)), ((), ())), precision=precision, preferred_element_type=F32)


def nn(a, b, precision=None):
    return jnp.dot(a, b, precision=precision, preferred_element_type=F32)


def iota(shape, dim):
    return lax.broadcasted_iota(jnp.int32, shape, dim)


def flag(mask):
    return jnp.where(mask, 1.0, 0.0).astype(F32)


def sort_slots(row, col, count, a):
    live = iota((1, SLOTS), 1) < count
    local = jnp.where(live, row - a * GROUP, 2 * GROUP - 1)
    owner = col >> 5
    part = col & 3
    oy, oz = owner >> 2, owner & 3
    piece = part >> 1
    place = jnp.where(piece == 0, oz * 4 + oy, oy * 4 + oz)
    tile = piece * 32 + place * 2 + (part & 1)
    local_f = local.astype(F32)
    row_t = jnp.broadcast_to(local_f, (BS, SLOTS)).T
    lane = iota((SLOTS, BS), 1).astype(F32)
    hits = flag(row_t == lane)
    counts = jnp.sum(hits, axis=0, keepdims=True)
    counts = jnp.where(iota((1, BS), 1) < GROUP, counts, 0.0)
    pairs = ((counts.astype(jnp.int32) + 1) >> 1).astype(F32)
    upper = flag(iota((BS, BS), 0) < iota((BS, BS), 1)).astype(BF16)
    start = nn(jnp.broadcast_to(pairs, (16, BS)).astype(BF16), upper)[:1]
    row_w = jnp.concatenate([row_t] * (SLOTS // BS), axis=1)
    before = (row_w == local_f) & (iota((SLOTS, SLOTS), 1) < iota((SLOTS, SLOTS), 0))
    within = jnp.sum(flag(before), axis=1, keepdims=True)
    base = jnp.sum(hits * start, axis=1, keepdims=True)
    pos = 2.0 * base + within
    pos = jnp.where(row_t[:, :1] < GROUP, pos, 4096.0)
    onehot = flag(pos == iota((SLOTS, 512), 1).astype(F32)).astype(BF16)
    slot = iota((1, SLOTS), 1)
    values = jnp.concatenate(
        [(slot >> 4).astype(F32), (slot & 15).astype(F32), tile.astype(F32), jnp.ones((1, SLOTS), F32),
         jnp.zeros((12, SLOTS), F32)], axis=0).astype(BF16)
    placed = nn(values, onehot)
    perm = placed[0:1] * 16.0 + placed[1:2] + SLOTS * (1.0 - placed[3:4])
    start_t = jnp.broadcast_to(start, (BS, BS)).T
    pairs_t = jnp.broadcast_to(pairs, (BS, BS)).T
    lane4 = iota((BS, 512), 1).astype(F32)
    first = jnp.sum(flag((start_t[:, :1] == lane4) & (pairs_t[:, :1] > 0.0)), axis=0, keepdims=True)
    pad = jnp.zeros((1, 512 - BS), F32)
    last = jnp.concatenate([jnp.maximum(start + pairs - 1.0, 0.0), pad], axis=1)
    filled = jnp.concatenate([jnp.minimum(pairs, 1.0), pad], axis=1)
    ints = jnp.concatenate([perm, placed[2:3], last, jnp.zeros((5, 512), F32)], axis=0).astype(jnp.int32)
    floats = jnp.concatenate([1.0 - first, filled, jnp.zeros((6, 512), F32)], axis=0)
    return ints, floats


def apply_kernel(x_ref, w_hbm, row_ref, col_ref, cnt_ref, lap_ref, amat_ref, bmat_ref,
                 w_ref, slab1, slab2, prod, xt_ref, ints_v, floats_v, ints_s, floats_s,
                 sib1_s, sib1_r, sib2_s, sib2_r, hi_s, hi_r, lo_s, lo_r, deg_s, deg_r, q_s, q_r,
                 own1, own2, deg_ref,
                 a_part, a_r1, a_b2, a_b3, b_part, b_r1, b_b2, b_b3,
                 send_sem, recv_sem, local_sem):
    a = lax.axis_index("rows")
    b = lax.axis_index("cols")
    y, z = a // NZ, a % NZ
    xx, core = b // 2, b % 2
    counter = [0]

    def ydev(d):
        return {"rows": ((y + d + NY) % NY) * NZ + z, "cols": b}

    def zdev(d):
        return {"rows": y * NZ + (z + d + NZ) % NZ, "cols": b}

    def coldev(d):
        return {"rows": a, "cols": (b + d) % NCOL}

    def xdev(d):
        return {"rows": a, "cols": ((xx + d) % NX) * 2 + core}

    sibling = {"rows": a, "cols": xx * 2 + (1 - core)}
    sent = []

    def send(src, dst, device):
        k = counter[0]
        counter[0] += 1
        copy = pltpu.make_async_remote_copy(
            src_ref=src, dst_ref=dst, send_sem=send_sem.at[k], recv_sem=recv_sem.at[k],
            device_id=device, device_id_type=pl.DeviceIdType.MESH)
        copy.start()
        sent.append(copy)
        return copy

    w_copy = pltpu.make_async_copy(w_hbm, w_ref.at[pl.ds(0, SLOTS)], local_sem.at[0])
    w_copy.start()

    barrier = pltpu.get_barrier_semaphore()
    partners = [coldev(d) for d in range(1, NCOL)] + [ydev(d) for d in (1, 2, 3)] + [zdev(d) for d in (1, 2, 3)]
    for device in partners:
        pl.semaphore_signal(barrier, inc=1, device_id=device, device_id_type=pl.DeviceIdType.MESH)

    place = ((z, y), (y, z))

    def span(p, i, j, size):
        return pl.ds(p * 32 + (i * 4 + j) * 2, size)

    for r in range(4):
        xt = x_ref[r * BS:(r + 1) * BS, :].astype(F32).T
        xt_ref[r] = xt
        p, t = r // 2, r % 2
        slab1[p * 32 + (place[p][0] * 4 + place[p][1]) * 2 + t] = xt.astype(BF16)

    pl.semaphore_wait(barrier, len(partners))

    def gather(slab):
        def first(p, d):
            return ydev(d) if p == 0 else zdev(d)

        def second(p, d):
            return zdev(d) if p == 0 else ydev(d)

        near = []
        for p in range(2):
            i, j = place[p]
            own = slab.at[span(p, i, j, 2)]
            near.append((send(own, own, first(p, 1)), send(own, own, first(p, -1))))
        yield
        far = []
        for p in range(2):
            i, j = place[p]
            near[p][0].wait_recv()
            one = slab.at[span(p, i, (j + 3) % 4, 1)]
            fwd_r = send(one, one, first(p, 1))
            near[p][1].wait_recv()
            two = slab.at[pl.ds(p * 32 + (i * 4 + (j + 1) % 4) * 2 + 1, 1)]
            fwd_l = send(two, two, first(p, -1))
            far.append((fwd_r, fwd_l))
        yield
        wide = []
        for p in range(2):
            i, j = place[p]
            far[p][0].wait_recv()
            far[p][1].wait_recv()
            low = slab.at[span(p, i, 0, 4)]
            high = slab.at[span(p, i, 2, 4)]
            low_r = send(low, low, second(p, 1))
            high_l = send(high, high, second(p, -1))
            high_r = send(high, high, second(p, 1))
            low_l = send(low, low, second(p, -1))
            wide.append((low_r, high_l, high_r, low_l))
        yield
        rest = []
        for p in range(2):
            i, j = place[p]
            wide[p][0].wait_recv()
            low = slab.at[span(p, (i + 3) % 4, 0, 4)]
            rest.append(send(low, low, second(p, 1)))
            wide[p][1].wait_recv()
            high = slab.at[span(p, (i + 1) % 4, 2, 4)]
            rest.append(send(high, high, second(p, -1)))
        yield
        for p in range(2):
            wide[p][2].wait_recv()
            wide[p][3].wait_recv()
        for copy in rest:
            copy.wait_recv()
        yield

    g1 = gather(slab1)
    next(g1)
    w_ref[SLOTS] = jnp.zeros((BS, BS), BF16)
    ints, floats = sort_slots(row_ref[...], col_ref[...], cnt_ref[0, 0], a)
    ints_v[...] = ints
    floats_v[...] = floats
    ints_copy = pltpu.make_async_copy(ints_v, ints_s, local_sem.at[1])
    floats_copy = pltpu.make_async_copy(floats_v, floats_s, local_sem.at[2])
    ints_copy.start()
    floats_copy.start()
    next(g1)
    next(g1)
    ints_copy.wait()
    floats_copy.wait()
    next(g1)
    xx_mat = sum(nt(xt_ref[r].astype(BF16), xt_ref[r].astype(BF16)) for r in range(4))
    a_part[:, 0] = xx_mat.reshape(8, 16, BS)
    w_copy.wait()
    next(g1)

    def pick(kind, at, top):
        return jnp.clip(ints_s[kind, at], 0, top)

    def product(slab, with_degree):
        rows = BS + DEG if with_degree else BS
        ones = jnp.ones((16, 2 * BS), BF16)

        def body(n, acc):
            for u in range(UNROLL):
                s = n * UNROLL + u
                left = jnp.concatenate([slab[pick(1, 2 * s, 63)], slab[pick(1, 2 * s + 1, 63)]], axis=1)
                if with_degree:
                    left = jnp.concatenate([left, ones], axis=0)
                right = jnp.concatenate([w_ref[pick(0, 2 * s, SLOTS)], w_ref[pick(0, 2 * s + 1, SLOTS)]], axis=1)
                acc = acc * floats_s[0, s] + nt(left, right)[:rows]
                prod[s, :rows] = acc
            return acc

        lax.fori_loop(0, PAIRS // UNROLL, body, jnp.zeros((rows, BS), F32))

    def tile(g, rows):
        return prod[pick(2, g, PAIRS - 1), :rows] * floats_s[1, g]

    def order(d):
        return (xx + d) % NX

    product(slab1, True)
    rows = BS + DEG
    from_sib = {}
    for d in (2, 1, 3, 0):
        for r in range(4):
            sib1_s[d, r] = tile((order(d) * 2 + (1 - core)) * 4 + r, rows)
        from_sib[d] = send(sib1_s.at[d], sib1_r.at[d], sibling)
    hi_copy, deg_copy = {}, {}
    for d in (2, 1, 3, 0):
        from_sib[d].wait_recv()
        for r in range(4):
            total = tile((order(d) * 2 + core) * 4 + r, rows) + sib1_r[d, r]
            if d:
                high = total[:BS].astype(BF16)
                hi_s[d - 1, r] = high
                lo_s[d - 1, r] = (total[:BS] - high.astype(F32)).astype(BF16)
                deg_s[d - 1, r] = total[BS:]
            else:
                own1[r] = total[:BS]
                deg_ref[r] = total[BS:]
        if d:
            deg_copy[d] = send(deg_s.at[d - 1], deg_r.at[d - 1], xdev(d))
            hi_copy[d] = send(hi_s.at[d - 1], hi_r.at[d - 1], xdev(d))
    for d in (1, 3, 2):
        deg_copy[d].wait_recv()
        hi_copy[d].wait_recv()
    for r in range(4):
        degree = deg_ref[r] + deg_r[0, r] + deg_r[1, r] + deg_r[2, r]
        deg_ref[r] = degree
        spread = jnp.broadcast_to(degree[:1], (BS, BS))
        summed = own1[r] + hi_r[0, r].astype(F32) + hi_r[1, r].astype(F32) + hi_r[2, r].astype(F32)
        lap = spread * xt_ref[r] - summed
        own1[r] = lap
        p, t = r // 2, r % 2
        slab2[p * 32 + (place[p][0] * 4 + place[p][1]) * 2 + t] = lap.astype(BF16)
    g2 = gather(slab2)
    next(g2)
    lo_copy = {d: send(lo_s.at[d - 1], lo_r.at[d - 1], xdev(d)) for d in (2, 1, 3)}
    next(g2)
    next(g2)
    for d in (1, 3, 2):
        lo_copy[d].wait_recv()
    for r in range(4):
        lap_ref[r] = own1[r] - (lo_r[0, r].astype(F32) + lo_r[1, r].astype(F32) + lo_r[2, r].astype(F32))

    def joined(ref):
        return jnp.concatenate([ref[r] for r in range(4)], axis=1)

    def all_reduce(part, r1, b2, b3, res):
        copies = [send(part.at[(b + d) % NCOL], r1.at[d - 1], coldev(d)) for d in range(1, NCOL)]
        yield
        for copy in copies:
            copy.wait_recv()
        total = part[b]
        for d in range(1, NCOL):
            total = total + r1[d - 1]
        b2[y] = total
        copies = [send(b2.at[y], b2.at[y], ydev(d)) for d in (1, 2, 3)]
        yield
        for copy in copies:
            copy.wait_recv()
        b3[z] = b2[0] + b2[1] + b2[2] + b2[3]
        copies = [send(b3.at[z], b3.at[z], zdev(d)) for d in (1, 2, 3)]
        yield
        for copy in copies:
            copy.wait_recv()
        res[b] = b3[0] + b3[1] + b3[2] + b3[3]
        copies = [send(res.at[b], res.at[b], coldev(d)) for d in range(1, NCOL)]
        yield
        for copy in copies:
            copy.wait_recv()
        yield

    lap_all = joined(lap_ref)
    a_part[:, 1] = nt(joined(xt_ref), lap_all, HI).reshape(8, 16, BS)
    a_part[:, 2] = nt(lap_all, lap_all, HI).reshape(8, 16, BS)
    next(g2)
    reduce_a = all_reduce(a_part, a_r1, a_b2, a_b3, amat_ref)
    next(reduce_a)
    next(reduce_a)
    next(g2)
    next(reduce_a)

    product(slab2, False)
    from_sib = {}
    for d in (2, 1, 3, 0):
        for r in range(4):
            sib2_s[d, r] = tile((order(d) * 2 + (1 - core)) * 4 + r, BS).astype(BF16)
        from_sib[d] = send(sib2_s.at[d], sib2_r.at[d], sibling)
    q_copy = {}
    for d in (2, 1, 3, 0):
        from_sib[d].wait_recv()
        for r in range(4):
            total = tile((order(d) * 2 + core) * 4 + r, BS) + sib2_r[d, r].astype(F32)
            if d:
                q_s[d - 1, r] = total.astype(BF16)
            else:
                own2[r] = total
        if d:
            q_copy[d] = send(q_s.at[d - 1], q_r.at[d - 1], xdev(d))
    next(reduce_a)
    for d in (1, 3, 2):
        q_copy[d].wait_recv()
    for r in range(4):
        spread = jnp.broadcast_to(deg_ref[r][:1], (BS, BS))
        summed = own2[r] + q_r[0, r].astype(F32) + q_r[1, r].astype(F32) + q_r[2, r].astype(F32)
        own2[r] = spread * lap_ref[r] - summed
    y_all = joined(own2)
    b_part[:, 0] = nt(joined(xt_ref), y_all, HI).reshape(8, 16, BS)
    b_part[:, 1] = nt(joined(lap_ref), y_all, HI).reshape(8, 16, BS)
    reduce_b = all_reduce(b_part, b_r1, b_b2, b_b3, bmat_ref)
    next(reduce_b)
    next(reduce_a)
    for unused in range(4):
        next(reduce_b)
    for copy in sent:
        copy.wait_send()


def factor_inverse(gram):
    left = [gram[8 * i:8 * i + 8] for i in range(16)]
    right = [flag(iota((8, BS), 1) == iota((8, BS), 0) + 8 * i) for i in range(16)]
    sub = iota((8, 1), 0)
    out = []
    for k in range(16):
        scale = jnp.zeros((8, 1), F32)
        for j in range(8):
            c = 8 * k + j
            root = lax.rsqrt(left[k][j:j + 1, c:c + 1])
            inv = root * root
            scale = jnp.where(sub == j, root, scale)
            lrow = left[k][j:j + 1] * inv
            rrow = right[k][j:j + 1] * inv
            for i in range(k, 16):
                f = left[i][:, c:c + 1]
                if i == k:
                    f = jnp.where(sub > j, f, 0.0)
                left[i] = left[i] - f * lrow
                right[i] = right[i] - f * rrow
        out.append(right[k] * scale)
    return jnp.concatenate(out, axis=0)


def finish_kernel(inverse, x_ref, lap_ref, amat_ref, bmat_ref, search_ref, proj_ref):
    def mat(ref, m):
        return ref[:, m].reshape(BS, BS) * inverse

    g, theta, s = mat(amat_ref, 0), mat(amat_ref, 1), mat(amat_ref, 2)
    m = 2.0 * theta - nn(g, theta, HI)
    m_t = m.T
    cross = nn(m_t, theta, HI)
    gram = s - cross.T - cross + nn(m_t, nn(g, m, HI), HI)
    t_t = factor_inverse(gram)
    mt_t = nt(t_t, m, HI)
    x_f = x_ref[...].astype(F32)
    for r in range(4):
        part = nn(t_t, lap_ref[r], HI) - nt(mt_t, x_f[r * BS:(r + 1) * BS], HI)
        search_ref[r * BS:(r + 1) * BS, :] = part.T.astype(BF16)
    q1 = mat(bmat_ref, 0) - nn(theta, m, HI)
    q2 = mat(bmat_ref, 1) - nn(s, m, HI) - nn(m_t, q1, HI)
    proj_ref[:BS, :BS] = theta
    proj_ref[:BS, BS:] = nt(q1, t_t, HI)
    proj_ref[BS:, :BS] = nn(t_t, s - cross, HI)
    proj_ref[BS:, BS:] = nt(nn(t_t, q2, HI), t_t, HI)


def shards(iterate, blocks, block_row, block_col, block_count):
    vmem = pl.BlockSpec(memory_space=pltpu.VMEM)
    shape = jax.ShapeDtypeStruct
    rows1 = BS + DEG

    def sds(*dims, dtype=F32):
        return pltpu.VMEM(dims, dtype)

    lap, amat, bmat = pl.pallas_call(
        apply_kernel,
        out_shape=(shape((4, BS, BS), F32), shape((8, 3, 16, BS), F32), shape((8, 2, 16, BS), F32)),
        in_specs=[vmem, pl.BlockSpec(memory_space=pl.ANY), vmem, vmem,
                  pl.BlockSpec(memory_space=pltpu.SMEM)],
        out_specs=(vmem, vmem, vmem),
        scratch_shapes=[
            sds(SLOTS + 1, BS, BS, dtype=BF16), sds(64, BS, BS, dtype=BF16), sds(64, BS, BS, dtype=BF16),
            sds(PAIRS, rows1, BS), sds(4, BS, BS), sds(8, 512, dtype=jnp.int32), sds(8, 512),
            pltpu.SMEM((8, 512), jnp.int32), pltpu.SMEM((8, 512), F32),
            sds(4, 4, rows1, BS), sds(4, 4, rows1, BS),
            sds(4, 4, BS, BS, dtype=BF16), sds(4, 4, BS, BS, dtype=BF16),
            sds(3, 4, BS, BS, dtype=BF16), sds(3, 4, BS, BS, dtype=BF16),
            sds(3, 4, BS, BS, dtype=BF16), sds(3, 4, BS, BS, dtype=BF16),
            sds(3, 4, DEG, BS), sds(3, 4, DEG, BS),
            sds(3, 4, BS, BS, dtype=BF16), sds(3, 4, BS, BS, dtype=BF16),
            sds(4, BS, BS), sds(4, BS, BS), sds(4, DEG, BS),
            sds(8, 3, 16, BS), sds(7, 3, 16, BS), sds(4, 3, 16, BS), sds(4, 3, 16, BS),
            sds(8, 2, 16, BS), sds(7, 2, 16, BS), sds(4, 2, 16, BS), sds(4, 2, 16, BS),
            pltpu.SemaphoreType.DMA((N_SEM,)), pltpu.SemaphoreType.DMA((N_SEM,)), pltpu.SemaphoreType.DMA((3,)),
        ],
        compiler_params=pltpu.CompilerParams(
            collective_id=0, has_side_effects=True, vmem_limit_bytes=60 * 1024 * 1024),
        name="apply_twice",
    )(iterate, blocks.reshape(SLOTS, BS, BS), block_row.reshape(1, SLOTS), block_col.reshape(1, SLOTS),
      block_count.reshape(1, 1))
    node_total = iterate.shape[0] * lax.axis_size("rows") * lax.axis_size("cols")

    def finish(*refs):
        finish_kernel(1.0 / node_total, *refs)

    return pl.pallas_call(
        finish,
        out_shape=(shape(iterate.shape, BF16), shape((2 * BS, 2 * BS), F32)),
        in_specs=[vmem] * 4,
        out_specs=(vmem, vmem),
        compiler_params=pltpu.CompilerParams(vmem_limit_bytes=32 * 1024 * 1024),
        name="finish",
    )(iterate, lap, amat, bmat)


def solution(mesh):
    placed = (
        P(("rows", "cols"), None),
        P("rows", "cols", None, None, None),
        P("rows", "cols", None),
        P("rows", "cols", None),
        P("rows", "cols"),
    )
    return jax.shard_map(
        shards,
        mesh=mesh,
        in_specs=placed,
        out_specs=(P(("rows", "cols"), None), P()),
        check_vma=False,
    )
```

time: 931 us -> 117 us (0.13)
  waiting for transfers between devices: 685 us -> 0 us
  Pallas kernels: 0 us -> 112 us
  matrix products: 84.8 us -> 0 us
  local copies, waits for them, and re-layouts: 85.6 us -> 2.78 us
  other arithmetic: 35.3 us -> 0 us
  blocking collectives: 22.7 us -> 0 us
  between operations: 15.6 us -> 1.35 us
    psum x4 -> x0, waiting for transfers between devices: 565 us -> none  [the longest x1 147 us: shards(): lax.psum((cross_xq, cross_qx, inner_qq), ('rows', 'cols'))]
    pallas_call x0 -> x2, Pallas kernels: none -> 112 us  [the longest x1 98 us: shards(): pl.pallas_call(apply_kernel, out_shape=(shape((4, BS, BS), F32), shape((8...]
    all_gather x2 -> x0, waiting for transfers between devices: 91.3 us -> none  [the longest x1 47.6 us: shards(): iterate_slab = lax.all_gather(iterate, 'rows', axis=0, tiled=True)]
    dot_general x13 -> x0, matrix products: 83.7 us -> none  [the longest x2 44.2 us: apply_local(): jnp.einsum('nab,nbk->nak', values, picked, preferred_element_type=jnp.flo...]
    dot_general x3 -> x0, local copies, waits for them, and re-layouts: 50.7 us -> none  [the longest x2 49.5 us: apply_local(): jnp.einsum('nab,nbk->nak', values, picked, preferred_element_type=jnp.flo...]
    reduce_scatter x2 -> x0, waiting for transfers between devices: 28.4 us -> none  [the longest x1 28.4 us: shards(): lax.psum_scatter(adj_part.astype(jnp.bfloat16), 'cols', scatter_dimension...]
    gather x2 -> x0, local copies, waits for them, and re-layouts: 24.3 us -> none  [apply_local(): picked = tile_set[slab_index]]
    another operation x5 -> x0, other arithmetic: 22.9 us -> none  [the longest x3 12.4 us: shards(): lower_factor = jnp.linalg.cholesky(gram_mat)]
  transfers between devices with their start and end apart: 8 -> 0, of which waited for: 7 -> 0; matrix products, arithmetic and copies ran while one was open for 1% -> 0% of each run, Pallas kernels for 0% -> 0%
where the time goes in v1:
time: 117 us; the launch traced here: 116 us
  Pallas kernels  112 us (96%)
  local copies, waits for them, and re-layouts  2.78 us (2%)
  between operations  1.35 us (1%)
    pallas_call x1, Pallas kernels, shards(): pl.pallas_call(apply_kernel, out_shape=(shape((4, BS, BS), F32), shape((8...  98 us
    pallas_call x1, Pallas kernels, shards(): pl.pallas_call(finish, out_shape=(shape(iterate.shape, BF16), shape((2 *...  14.3 us
    unnamed x8, local copies, waits for them, and re-layouts  2.78 us

profile of v1, /device:TPU:1, one launch (start us, length us, event | category | flops | bytes accessed | tf_op | source)
XLA Modules:
  0.0 116.4 jit_solution(12853743886410130510)
XLA Ops:
  0.6 0.0 copy-start
  1.3 98.0 %apply_twice.1 = (f32[4,128,128]{2,1,0:T(8,128)}, f32[8,3,16,128]{3,2,1,0:T(8,128)}, f32[8,2,16,128]{3,2,1,0:T(8,128)}) custom-call(bf16[512,128]{1,0:T(8,128)(2,1)} %refs_0_.1, bf16[384,128,128]{2,1,0:T(8,128)(2,1)} %bitcast.3, s32[1,384]{1,0:T(1,128)} %bitcast.4, s32[1,384]{1,0:T(1,128)} %bitcast.5, s32[1,1]{1,0:T(1,128)S(6)} %copy.7.cnt_ref), custom_call_target="tpu_custom_call" | custom-call | tf_op jit(solution)/shard_map/apply_twice/pallas_call | solution.py:416
  99.3 0.0 copy-done
  99.4 0.0 copy-start.1
  99.4 0.9 copy-done.1
  100.3 0.0 copy-start.2
  100.3 0.9 copy-done.2
  101.2 0.0 copy-start.3
  101.2 0.9 copy-done.3
  102.1 14.3 %finish.1 = (bf16[512,128]{1,0:T(8,128)(2,1)}, f32[256,256]{1,0:T(8,128)}) custom-call(bf16[512,128]{1,0:T(8,128)(2,1)S(1)} %copy-done, f32[4,128,128]{2,1,0:T(8,128)S(1)} %copy-done.1, f32[8,3,16,128]{3,2,1,0:T(8,128)S(1)} %copy-done.2, f32[8,2,16,128]{3,2,1,0:T(8,128)S(1)} %copy-done.3), custom_call_target="tpu_custom_call" | custom-call | tf_op jit(solution)/shard_map/finish/pallas_call | solution.py:447
Async XLA Ops:
  0.6 98.7 %copy-start = (bf16[512,128]{1,0:T(8,128)(2,1)S(1)}, bf16[512,128]{1,0:T(8,128)(2,1)}, u32[]{:S(2)}) copy-start(bf16[512,128]{1,0:T(8,128)(2,1)} %refs_0_.1) | copy-start | bytes 393220
  99.4 1.0 copy-start.1
  100.3 0.9 copy-start.2
  101.2 0.9 copy-start.3

commit v2 on v0

v2 whole, which is shorter than its diff:
```python
import math

import jax
import jax.numpy as jnp
from jax import lax
from jax.experimental import pallas as pl
from jax.experimental.pallas import tpu as pltpu
from jax.sharding import PartitionSpec as P

BS = 128
NY = 4
NZ = 4
NX = 4
NCOL = 8
GROUP = 32
SLOTS = 384
PAIRS = (SLOTS + GROUP) // 2
UNROLL = 52
PART = 96
DEG = 8
N_SEM = 120
HALF = BS // 2
BLOCK_BYTES = BS * BS * 2

F32 = jnp.float32
BF16 = jnp.bfloat16
HI = lax.Precision.HIGHEST


def nt(a, b, precision=None):
    return lax.dot_general(a, b, (((1,), (1,)), ((), ())), precision=precision, preferred_element_type=F32)


def nn(a, b, precision=None):
    return jnp.dot(a, b, precision=precision, preferred_element_type=F32)


def iota(shape, dim):
    return lax.broadcasted_iota(jnp.int32, shape, dim)


def flag(mask):
    return jnp.where(mask, 1.0, 0.0).astype(F32)


def sort_slots(row, col, count, a):
    live = iota((1, SLOTS), 1) < count
    local = jnp.where(live, row - a * GROUP, 2 * GROUP - 1)
    owner = col >> 5
    part = col & 3
    oy, oz = owner >> 2, owner & 3
    piece = part >> 1
    place = jnp.where(piece == 0, oz * 4 + oy, oy * 4 + oz)
    tile = piece * 32 + place * 2 + (part & 1)
    local_f = local.astype(F32)
    row_t = jnp.broadcast_to(local_f, (BS, SLOTS)).T
    lane = iota((SLOTS, BS), 1).astype(F32)
    hits = flag(row_t == lane)
    counts = jnp.sum(hits, axis=0, keepdims=True)
    counts = jnp.where(iota((1, BS), 1) < GROUP, counts, 0.0)
    pairs = ((counts.astype(jnp.int32) + 1) >> 1).astype(F32)
    upper = flag(iota((BS, BS), 0) < iota((BS, BS), 1)).astype(BF16)
    start = nn(jnp.broadcast_to(pairs, (16, BS)).astype(BF16), upper)[:1]
    row_w = jnp.concatenate([row_t] * (SLOTS // BS), axis=1)
    before = (row_w == local_f) & (iota((SLOTS, SLOTS), 1) < iota((SLOTS, SLOTS), 0))
    within = jnp.sum(flag(before), axis=1, keepdims=True)
    base = jnp.sum(hits * start, axis=1, keepdims=True)
    pos = 2.0 * base + within
    pos = jnp.where(row_t[:, :1] < GROUP, pos, 4096.0)
    onehot = flag(pos == iota((SLOTS, 512), 1).astype(F32)).astype(BF16)
    slot = iota((1, SLOTS), 1)
    values = jnp.concatenate(
        [(slot >> 4).astype(F32), (slot & 15).astype(F32), tile.astype(F32), jnp.ones((1, SLOTS), F32),
         jnp.zeros((12, SLOTS), F32)], axis=0).astype(BF16)
    placed = nn(values, onehot)
    perm = placed[0:1] * 16.0 + placed[1:2] + SLOTS * (1.0 - placed[3:4])
    start_t = jnp.broadcast_to(start, (BS, BS)).T
    pairs_t = jnp.broadcast_to(pairs, (BS, BS)).T
    lane4 = iota((BS, 512), 1).astype(F32)
    first = jnp.sum(flag((start_t[:, :1] == lane4) & (pairs_t[:, :1] > 0.0)), axis=0, keepdims=True)
    pad = jnp.zeros((1, 512 - BS), F32)
    last = jnp.concatenate([jnp.maximum(start + pairs - 1.0, 0.0), pad], axis=1)
    filled = jnp.concatenate([jnp.minimum(pairs, 1.0), pad], axis=1)
    ints = jnp.concatenate([perm, placed[2:3], last, jnp.zeros((5, 512), F32)], axis=0).astype(jnp.int32)
    floats = jnp.concatenate([1.0 - first, filled, jnp.zeros((6, 512), F32)], axis=0)
    return ints, floats


def factor_inverse(gram):
    left = [gram[8 * i:8 * i + 8] for i in range(16)]
    right = [flag(iota((8, BS), 1) == iota((8, BS), 0) + 8 * i) for i in range(16)]
    sub = iota((8, BS), 0)
    out = []

    def wide(v):
        return jnp.broadcast_to(v, (8, BS))

    for k in range(16):
        c = 8 * k
        lanes = [wide(left[k][:, c + n:c + n + 1]) for n in range(8)]
        elem = [[wide(lanes[n][j:j + 1]) if n <= j else None for n in range(8)] for j in range(8)]
        inv = [[None] * 8 for unused in range(8)]
        roots, pivots = [], []
        for j in range(8):
            root = lax.rsqrt(elem[j][j])
            roots.append(root)
            pivot = root * root
            pivots.append(pivot)
            mult = [elem[i][j] * pivot if i > j else None for i in range(8)]
            for i in range(j + 1, 8):
                for n in range(j + 1, i + 1):
                    elem[i][n] = elem[i][n] - mult[i] * elem[n][j]
                for n in range(j):
                    inv[i][n] = inv[i][n] - mult[i] * inv[j][n]
                inv[i][j] = -mult[i]
        lrows = [wide(left[k][j:j + 1]) for j in range(8)]
        rrows = [wide(right[k][j:j + 1]) for j in range(8)]

        def solved(rows):
            first = []
            for j in range(8):
                total = rows[j]
                for n in range(j):
                    total = total + inv[j][n] * rows[n]
                first.append(total)
            scaled = [first[j] * pivots[j] for j in range(8)]
            second = []
            for j in range(8):
                total = scaled[j]
                for n in range(j + 1, 8):
                    total = total + inv[n][j] * scaled[n]
                second.append(total)
            return first, second

        unused, lsol = solved(lrows)
        rfirst, rsol = solved(rrows)
        for i in range(k + 1, 16):
            for j in range(8):
                f = wide(left[i][:, c + j:c + j + 1])
                left[i] = left[i] - f * lsol[j]
                right[i] = right[i] - f * rsol[j]
        rows = jnp.zeros((8, BS), F32)
        for j in range(8):
            rows = jnp.where(sub == j, rfirst[j] * roots[j], rows)
        out.append(rows)
        if k in (3, 11):
            yield None
    yield jnp.concatenate(out, axis=0)


def step_kernel(inverse, x_hbm, w_hbm, row_hbm, col_hbm, cnt_ref, search_hbm, proj_hbm,
                x_ref, row_ref, col_ref, search_ref, proj_ref, w_ref,
                slab1a, slab1b, slab2a, slab2b, prod, xt_ref, ints_v, floats_v, ints_s, floats_s,
                siba_s, siba_r, sibb_s, sibb_r, hi_s, hi_r, lo_s, lo_r, deg_s, deg_r,
                lap_ref, deg_ref, x_group, l_group,
                a_part, a_r1, a_b2, a_b3, a_res, b_part, b_r1, b_b2, b_res,
                send_sem, recv_sem, local_sem):
    slab1, slab2 = (slab1a, slab1b), (slab2a, slab2b)
    sib_s, sib_r = (siba_s, sibb_s), (siba_r, sibb_r)
    a = lax.axis_index("rows")
    b = lax.axis_index("cols")
    y, z = a // NZ, a % NZ
    xx, core = b // 2, b % 2
    counter = [0]

    def ydev(d):
        return {"rows": ((y + d + NY) % NY) * NZ + z, "cols": b}

    def zdev(d):
        return {"rows": y * NZ + (z + d + NZ) % NZ, "cols": b}

    def yzdev(d):
        return {"rows": ((y + d // NZ) % NY) * NZ + (z + d % NZ) % NZ, "cols": b}

    def coldev(d):
        return {"rows": a, "cols": (b + d) % NCOL}

    def xdev(d):
        return {"rows": a, "cols": ((xx + d) % NX) * 2 + core}

    sibling = {"rows": a, "cols": xx * 2 + (1 - core)}
    sent = [0]

    def new_sem():
        counter[0] += 1
        return counter[0] - 1

    def remote(src, dst, device, k):
        return pltpu.make_async_remote_copy(
            src_ref=src, dst_ref=dst, send_sem=send_sem.at[0], recv_sem=recv_sem.at[k],
            device_id=device, device_id_type=pl.DeviceIdType.MESH)

    def send(src, dst, device, k=None):
        copy = remote(src, dst, device, new_sem() if k is None else k)
        copy.start()
        sent[0] += math.prod(src.shape) * src.dtype.itemsize
        return copy

    def wait_bytes(like, k):
        remote(like, like, sibling, k).wait_recv()

    barrier = pltpu.get_barrier_semaphore()
    partners = [coldev(d) for d in range(1, NCOL)] + [yzdev(d) for d in range(1, NY * NZ)]
    for device in partners:
        pl.semaphore_signal(barrier, inc=1, device_id=device, device_id_type=pl.DeviceIdType.MESH)

    x_copy = pltpu.make_async_copy(x_hbm, x_ref, local_sem.at[3])
    row_copy = pltpu.make_async_copy(row_hbm, row_ref, local_sem.at[4])
    col_copy = pltpu.make_async_copy(col_hbm, col_ref, local_sem.at[5])
    x_copy.start()
    row_copy.start()
    col_copy.start()
    w_copies = [pltpu.make_async_copy(w_hbm.at[pl.ds(n * PART, PART)], w_ref.at[pl.ds(n * PART, PART)],
                                      local_sem.at[6 + n]) for n in range(SLOTS // PART)]
    for copy in w_copies:
        copy.start()
    x_copy.wait()

    place = ((z, y), (y, z))

    def span(p, i, j, size):
        return pl.ds(p * 32 + (i * 4 + j) * 2, size)

    for r in range(4):
        xt = x_ref[r * BS:(r + 1) * BS, :].astype(F32).T
        xt_ref[r] = xt
        xt = xt.astype(BF16)
        x_group[core, xx, r] = xt
        p, t = r // 2, r % 2
        for h in range(2):
            slab1[h][p * 32 + (place[p][0] * 4 + place[p][1]) * 2 + t] = xt[h * HALF:(h + 1) * HALF]
    w_ref[SLOTS] = jnp.zeros((BS, BS), BF16)
    pl.semaphore_wait(barrier, len(partners))

    def gather(slab):
        def first(p, d):
            return ydev(d) if p == 0 else zdev(d)

        def second(p, d):
            return zdev(d) if p == 0 else ydev(d)

        def block(p, i, j):
            return slab.at[span(p, i, j, 2)]

        def half(p, i, j, t):
            return slab.at[pl.ds(p * 32 + (i * 4 + j) * 2 + t, 1)]

        def spread(p, j):
            i = place[p][0]
            ref = block(p, i, j)
            return send(ref, ref, second(p, 1)), send(ref, ref, second(p, -1))

        def pass_on(p, j, pair, k):
            i = place[p][0]
            pair[0].wait_recv()
            one = half(p, (i + 3) % 4, j, 0)
            send(one, one, second(p, 1), k)
            pair[1].wait_recv()
            two = half(p, (i + 1) % 4, j, 1)
            send(two, two, second(p, -1), k)

        near, own, side, far = [], [], [], []
        ends = new_sem()
        for p in range(2):
            i, j = place[p]
            ref = block(p, i, j)
            near.append((send(ref, ref, first(p, 1)), send(ref, ref, first(p, -1))))
        for p in range(2):
            i, j = place[p]
            ref = block(p, i, j)
            far.append(send(ref, ref, first(p, 2)))
        for p in range(2):
            own.append(spread(p, place[p][1]))
        yield
        for p in range(2):
            j = place[p][1]
            near[p][0].wait_recv()
            one = spread(p, (j + 3) % 4)
            near[p][1].wait_recv()
            side.append((one, spread(p, (j + 1) % 4)))
        yield
        for p in range(2):
            i, j = place[p]
            far[p].wait_recv()
            ref = block(p, i, (j + 2) % 4)
            for d in (2, 1, -1):
                send(ref, ref, second(p, d), ends)
        yield
        for p in range(2):
            pass_on(p, place[p][1], own[p], ends)
        yield
        for p in range(2):
            pass_on(p, (place[p][1] + 3) % 4, side[p][0], ends)
            pass_on(p, (place[p][1] + 1) % 4, side[p][1], ends)
        yield
        wait_bytes(slab.at[pl.ds(0, 24)], ends)
        yield

    def group_gather(buf):
        copies = [send(buf.at[core, xx], buf.at[core, xx], xdev(d)) for d in (2, 1, 3)]
        yield
        for copy in copies:
            copy.wait_recv()
        copy = send(buf.at[core], buf.at[core], sibling)
        yield
        copy.wait_recv()
        yield

    g1 = [gather(slab1[h]) for h in range(2)]
    next(g1[0])
    row_copy.wait()
    col_copy.wait()
    ints, floats = sort_slots(row_ref[...], col_ref[...], cnt_ref[0, 0], a)
    ints_v[...] = ints
    floats_v[...] = floats
    ints_copy = pltpu.make_async_copy(ints_v, ints_s, local_sem.at[1])
    floats_copy = pltpu.make_async_copy(floats_v, floats_s, local_sem.at[2])
    ints_copy.start()
    floats_copy.start()
    def flip(n):
        def body(s, carry):
            w_ref[s] = w_ref[s].T
            return carry

        w_copies[n].wait()
        lax.fori_loop(n * PART, (n + 1) * PART, body, 0, unroll=16)

    flip(0)
    next(g1[0])
    next(g1[1])
    flip(1)
    next(g1[0])
    next(g1[0])
    flip(2)
    next(g1[0])
    next(g1[1])
    flip(3)
    next(g1[1])
    next(g1[1])
    ints_copy.wait()
    floats_copy.wait()
    xx_mat = sum(nt(xt_ref[r].astype(BF16), xt_ref[r].astype(BF16)) for r in range(4))
    a_part[:, 0] = xx_mat.reshape(8, 16, BS)
    next(g1[0])

    def pick(kind, at, top):
        return jnp.clip(ints_s[kind, at], 0, top)

    def product(slab, h, with_degree, hooks):
        rows = HALF + DEG if with_degree else HALF
        ones = jnp.ones((16, 2 * BS), BF16)

        def body(n, acc):
            for u in range(UNROLL):
                s = n * UNROLL + u
                left = jnp.concatenate([slab[pick(1, 2 * s, 63)], slab[pick(1, 2 * s + 1, 63)]], axis=1)
                if with_degree:
                    left = jnp.concatenate([left, ones], axis=0)
                right = jnp.concatenate([w_ref[pick(0, 2 * s, SLOTS)], w_ref[pick(0, 2 * s + 1, SLOTS)]], axis=0)
                acc = acc * floats_s[0, s] + nn(left, right)[:rows]
                prod[h, s, :rows] = acc
            return acc

        acc = jnp.zeros((rows, BS), F32)
        at = 0
        for step, hook in hooks + [(PAIRS // UNROLL, None)]:
            acc = lax.fori_loop(at, step, body, acc)
            at = step
            if hook is not None:
                hook()

    def tile(h, g, rows):
        return prod[h, pick(2, g, PAIRS - 1), :rows] * floats_s[1, g]

    def order(d):
        return (xx + d) % NX

    def joined(ref):
        return jnp.concatenate([ref[r] for r in range(4)], axis=1)

    def halves(h):
        return pl.ds(h * HALF, HALF)

    from_sib, hi_copy, deg_copy, lo_copy = {}, {}, {}, {}

    def reduce_start(h):
        rows = HALF + DEG if h == 0 else HALF
        for d in (2, 1, 3, 0):
            for r in range(4):
                sib_s[h][d, r] = tile(h, (order(d) * 2 + (1 - core)) * 4 + r, rows)
            from_sib[h, d] = send(sib_s[h].at[d], sib_r[h].at[d], sibling)

    def reduce_middle(h):
        rows = HALF + DEG if h == 0 else HALF
        for d in (2, 1, 3, 0):
            from_sib[h, d].wait_recv()
            for r in range(4):
                total = tile(h, (order(d) * 2 + core) * 4 + r, rows) + sib_r[h][d, r]
                if d:
                    high = total[:HALF].astype(BF16)
                    hi_s[h, d - 1, r] = high
                    lo_s[h, d - 1, r] = (total[:HALF] - high.astype(F32)).astype(BF16)
                    if h == 0:
                        deg_s[d - 1, r] = total[HALF:]
                else:
                    lap_ref[r, halves(h)] = total[:HALF]
                    if h == 0:
                        deg_ref[r] = total[HALF:]
            if d:
                if h == 0:
                    deg_copy[d] = send(deg_s.at[d - 1], deg_r.at[d - 1], xdev(d))
                hi_copy[h, d] = send(hi_s.at[h, d - 1], hi_r.at[h, d - 1], xdev(d))

    def reduce_end(h):
        for d in (1, 3, 2):
            if h == 0:
                deg_copy[d].wait_recv()
            hi_copy[h, d].wait_recv()
        for r in range(4):
            if h == 0:
                deg_ref[r] = deg_ref[r] + deg_r[0, r] + deg_r[1, r] + deg_r[2, r]
            degree = jnp.broadcast_to(deg_ref[r][:1], (HALF, BS))
            summed = lap_ref[r, halves(h)] + sum(hi_r[h, d, r].astype(F32) for d in range(3))
            lap = degree * xt_ref[r, halves(h)] - summed
            lap_ref[r, halves(h)] = lap
            lap = lap.astype(BF16)
            l_group[core, xx, r, halves(h)] = lap
            p, t = r // 2, r % 2
            slab2[h][p * 32 + (place[p][0] * 4 + place[p][1]) * 2 + t] = lap

    def all_reduce(part, r1, b2, b3, res):
        sems = [new_sem() for unused in range(4)]
        for d in range(1, NCOL):
            send(part.at[(b + d) % NCOL], r1.at[d - 1], coldev(d), sems[0])
        yield
        wait_bytes(r1, sems[0])
        total = part[b]
        for d in range(1, NCOL):
            total = total + r1[d - 1]
        b2[y] = total
        for d in (1, 2, 3):
            send(b2.at[y], b2.at[y], ydev(d), sems[1])
        yield
        wait_bytes(b2.at[pl.ds(0, 3)], sems[1])
        b3[z] = b2[0] + b2[1] + b2[2] + b2[3]
        for d in (1, 2, 3):
            send(b3.at[z], b3.at[z], zdev(d), sems[2])
        yield
        wait_bytes(b3.at[pl.ds(0, 3)], sems[2])
        res[b] = b3[0] + b3[1] + b3[2] + b3[3]
        for d in range(1, NCOL):
            send(res.at[b], res.at[b], coldev(d), sems[3])
        yield
        wait_bytes(res.at[pl.ds(0, 7)], sems[3])
        yield

    xg = group_gather(x_group)
    next(xg)
    product(slab1[0], 0, True, [(1, lambda: next(g1[1]))])
    reduce_start(0)
    next(g1[1])

    def middle():
        reduce_middle(0)
        next(xg)

    product(slab1[1], 1, False, [(2, middle)])
    reduce_start(1)
    reduce_end(0)
    g2 = [gather(slab2[h]) for h in range(2)]
    next(g2[0])
    reduce_middle(1)
    next(g2[0])
    next(g2[0])
    reduce_end(1)
    next(g2[1])
    lap_all = joined(lap_ref)
    a_part[:, 1] = nt(joined(xt_ref), lap_all, HI).reshape(8, 16, BS)
    a_part[:, 2] = nt(lap_all, lap_all, HI).reshape(8, 16, BS)
    reduce_a = all_reduce(a_part, a_r1, a_b2, a_b3, a_res)
    next(reduce_a)
    lg = group_gather(l_group)
    next(lg)
    next(g2[0])
    next(g2[0])
    scaled = joined(lap_ref) * jnp.concatenate([jnp.broadcast_to(deg_ref[r][:1], (BS, BS)) for r in range(4)], axis=1)
    pair_rows = jnp.concatenate([joined(xt_ref), joined(lap_ref)], axis=0)
    b_part[...] = nt(scaled, pair_rows, HI).reshape(8, 16, 2 * BS)
    next(g2[1])
    next(g2[1])
    next(g2[1])
    next(reduce_a)
    next(g2[0])

    def early():
        next(g2[1])
        for h in range(2):
            for d in (2, 1, 3):
                lo_copy[h, d] = send(lo_s.at[h, d - 1], lo_r.at[h, d - 1], xdev(d))

    product(slab2[0], 0, False, [(1, early), (3, lambda: next(reduce_a))])
    next(lg)
    next(g2[1])
    next(reduce_a)
    product(slab2[1], 1, False, [])
    next(lg)
    next(xg)
    total = jnp.zeros((BS, 2 * BS), F32)
    for c in range(2):
        for k in range(4):
            for r in (0, 2):
                g = (k * 2 + c) * 4 + r
                part = jnp.concatenate(
                    [jnp.concatenate([tile(h, g, HALF), tile(h, g + 1, HALF)], axis=1) for h in range(2)], axis=0)
                top = jnp.concatenate([x_group[c, k, r], x_group[c, k, r + 1]], axis=1)
                low = jnp.concatenate([l_group[c, k, r], l_group[c, k, r + 1]], axis=1)
                total = total + nt(part.astype(BF16), jnp.concatenate([top, low], axis=0))
    b_part[...] = b_part[...] - total.reshape(8, 16, 2 * BS)
    sems_b = [new_sem() for unused in range(3)]
    for d in range(1, NCOL):
        send(b_part.at[(b + d) % NCOL], b_r1.at[d - 1], coldev(d), sems_b[0])
    next(reduce_a)
    def mat(m):
        return a_res[:, m].reshape(BS, BS) * inverse

    gx, theta, s_mat = mat(0), mat(1), mat(2)
    m = 2.0 * theta - nn(gx, theta, HI)
    m_t = m.T
    cross = nn(m_t, theta, HI)
    gram = s_mat - cross.T - cross + nn(m_t, nn(gx, m, HI), HI)
    factor = factor_inverse(gram)
    next(factor)
    wait_bytes(b_r1, sems_b[0])
    part = b_part[b]
    for d in range(1, NCOL):
        part = part + b_r1[d - 1]
    b_b2[a] = part
    for d in range(1, NY * NZ):
        send(b_b2.at[a], b_b2.at[a], yzdev(d), sems_b[1])
    next(factor)
    wait_bytes(b_b2.at[pl.ds(0, NY * NZ - 1)], sems_b[1])
    part = b_b2[0]
    for k in range(1, NY * NZ):
        part = part + b_b2[k]
    b_res[b] = part
    for d in range(1, NCOL):
        send(b_res.at[b], b_res.at[b], coldev(d), sems_b[2])
    t_t = next(factor)
    for h in range(2):
        for d in (1, 3, 2):
            lo_copy[h, d].wait_recv()
    mt_t = nt(t_t, m, HI)
    for r in range(4):
        low = [sum(lo_r[h, d, r].astype(F32) for d in range(3)) for h in range(2)]
        lap = lap_ref[r] - jnp.concatenate(low, axis=0)
        part = nn(t_t, lap, HI) - nn(mt_t, xt_ref[r], HI)
        search_ref[r * BS:(r + 1) * BS, :] = part.T.astype(BF16)
    search_copy = pltpu.make_async_copy(search_ref, search_hbm, local_sem.at[3])
    search_copy.start()
    e1 = nt(mt_t, theta, HI)
    e2 = nn(mt_t, s_mat, HI)
    tail = jnp.concatenate([t_t, -mt_t], axis=1)
    proj_ref[:BS, :BS] = theta
    proj_ref[BS:, :BS] = nn(t_t, s_mat - cross, HI)
    wait_bytes(b_res.at[pl.ds(0, 7)], sems_b[2])
    spun = nn(t_t, b_res[...].reshape(BS, 2 * BS) * inverse, HI)
    xq = spun[:, :BS] - e1
    qq = nt(jnp.concatenate([spun[:, BS:] - e2, xq], axis=1), tail, HI)
    proj_ref[:BS, BS:] = xq.T
    proj_ref[BS:, BS:] = qq.T
    proj_copy = pltpu.make_async_copy(proj_ref, proj_hbm, local_sem.at[4])
    proj_copy.start()
    assert counter[0] <= N_SEM
    whole = w_ref.at[pl.ds(0, sent[0] // BLOCK_BYTES)]
    assert sent[0] % BLOCK_BYTES == 0
    remote(whole, whole, sibling, 0).wait_send()
    search_copy.wait()
    proj_copy.wait()


def shards(iterate, blocks, block_row, block_col, block_count):
    shape = jax.ShapeDtypeStruct
    rows1 = HALF + DEG
    node_total = iterate.shape[0] * lax.axis_size("rows") * lax.axis_size("cols")

    def buf(*dims, dtype=F32):
        return pltpu.VMEM(dims, dtype)

    def kernel(*refs):
        step_kernel(1.0 / node_total, *refs)

    outs = (shape(iterate.shape, BF16), shape((2 * BS, 2 * BS), F32))
    hbm = pl.BlockSpec(memory_space=pl.ANY)
    search, projected = pl.pallas_call(
        kernel,
        out_shape=outs,
        in_specs=[hbm, hbm, hbm, hbm, pl.BlockSpec(memory_space=pltpu.SMEM)],
        out_specs=(hbm, hbm),
        scratch_shapes=[
            buf(4 * BS, BS, dtype=BF16), buf(1, SLOTS, dtype=jnp.int32), buf(1, SLOTS, dtype=jnp.int32),
            buf(4 * BS, BS, dtype=BF16), buf(2 * BS, 2 * BS),
            buf(SLOTS + 1, BS, BS, dtype=BF16),
            buf(64, HALF, BS, dtype=BF16), buf(64, HALF, BS, dtype=BF16),
            buf(64, HALF, BS, dtype=BF16), buf(64, HALF, BS, dtype=BF16),
            buf(2, PAIRS, rows1, BS), buf(4, BS, BS), buf(8, 512, dtype=jnp.int32), buf(8, 512),
            pltpu.SMEM((8, 512), jnp.int32), pltpu.SMEM((8, 512), F32),
            buf(4, 4, rows1, BS), buf(4, 4, rows1, BS), buf(4, 4, HALF, BS), buf(4, 4, HALF, BS),
            buf(2, 3, 4, HALF, BS, dtype=BF16), buf(2, 3, 4, HALF, BS, dtype=BF16),
            buf(2, 3, 4, HALF, BS, dtype=BF16), buf(2, 3, 4, HALF, BS, dtype=BF16),
            buf(3, 4, DEG, BS), buf(3, 4, DEG, BS),
            buf(4, BS, BS), buf(4, DEG, BS),
            buf(2, 4, 4, BS, BS, dtype=BF16), buf(2, 4, 4, BS, BS, dtype=BF16),
            buf(8, 3, 16, BS), buf(7, 3, 16, BS), buf(4, 3, 16, BS), buf(4, 3, 16, BS), buf(8, 3, 16, BS),
            buf(8, 16, 2 * BS), buf(7, 16, 2 * BS), buf(16, 16, 2 * BS), buf(8, 16, 2 * BS),
            pltpu.SemaphoreType.DMA((1,)), pltpu.SemaphoreType.DMA((N_SEM,)), pltpu.SemaphoreType.DMA((10,)),
        ],
        compiler_params=pltpu.CompilerParams(
            collective_id=0, has_side_effects=True, vmem_limit_bytes=60 * 1024 * 1024),
        name="lobpcg_step",
    )(iterate, blocks.reshape(SLOTS, BS, BS), block_row.reshape(1, SLOTS), block_col.reshape(1, SLOTS),
      block_count.reshape(1, 1))

    def hand_over(search_ref, projected_ref, search_out, projected_out, search_v, projected_v, sems):
        pairs = [(search_ref, search_v, search_out), (projected_ref, projected_v, projected_out)]
        reads = [pltpu.make_async_copy(src, mid, sems.at[n]) for n, (src, mid, dst) in enumerate(pairs)]
        writes = [pltpu.make_async_copy(mid, dst, sems.at[n + 2]) for n, (src, mid, dst) in enumerate(pairs)]
        for copy in reads:
            copy.start()
        for n in range(2):
            reads[n].wait()
            writes[n].start()
        for copy in writes:
            copy.wait()

    return pl.pallas_call(
        hand_over, out_shape=outs, in_specs=[hbm, hbm], out_specs=(hbm, hbm),
        scratch_shapes=[buf(4 * BS, BS, dtype=BF16), buf(2 * BS, 2 * BS), pltpu.SemaphoreType.DMA((4,))],
        name="hand_over",
    )(search, projected)


def solution(mesh):
    placed = (
        P(("rows", "cols"), None),
        P("rows", "cols", None, None, None),
        P("rows", "cols", None),
        P("rows", "cols", None),
        P("rows", "cols"),
    )
    return jax.shard_map(
        shards,
        mesh=mesh,
        in_specs=placed,
        out_specs=(P(("rows", "cols"), None), P()),
        check_vma=False,
    )
```

time: 931 us -> 87.5 us (0.09)
  waiting for transfers between devices: 685 us -> 0 us
  Pallas kernels: 0 us -> 86 us
  local copies, waits for them, and re-layouts: 85.6 us -> 0 us
  matrix products: 84.8 us -> 0 us
  other arithmetic: 35.3 us -> 0 us
  blocking collectives: 22.7 us -> 0 us
  between operations: 15.6 us -> 1.45 us
    psum x4 -> x0, waiting for transfers between devices: 565 us -> none  [the longest x1 147 us: shards(): lax.psum((cross_xq, cross_qx, inner_qq), ('rows', 'cols'))]
    all_gather x2 -> x0, waiting for transfers between devices: 91.3 us -> none  [the longest x1 47.6 us: shards(): iterate_slab = lax.all_gather(iterate, 'rows', axis=0, tiled=True)]
    pallas_call x0 -> x2, Pallas kernels: none -> 86 us  [the longest x1 84.2 us: shards(): pl.pallas_call(kernel, out_shape=outs, in_specs=[hbm, hbm, hbm, hbm, pl.B...]
    dot_general x13 -> x0, matrix products: 83.7 us -> none  [the longest x2 44.2 us: apply_local(): jnp.einsum('nab,nbk->nak', values, picked, preferred_element_type=jnp.flo...]
    dot_general x3 -> x0, local copies, waits for them, and re-layouts: 50.7 us -> none  [the longest x2 49.5 us: apply_local(): jnp.einsum('nab,nbk->nak', values, picked, preferred_element_type=jnp.flo...]
    reduce_scatter x2 -> x0, waiting for transfers between devices: 28.4 us -> none  [the longest x1 28.4 us: shards(): lax.psum_scatter(adj_part.astype(jnp.bfloat16), 'cols', scatter_dimension...]
    gather x2 -> x0, local copies, waits for them, and re-layouts: 24.3 us -> none  [apply_local(): picked = tile_set[slab_index]]
    another operation x5 -> x0, other arithmetic: 22.9 us -> none  [the longest x3 12.4 us: shards(): lower_factor = jnp.linalg.cholesky(gram_mat)]
  transfers between devices with their start and end apart: 8 -> 0, of which waited for: 7 -> 0; matrix products, arithmetic and copies ran while one was open for 1% -> 0% of each run, Pallas kernels for 0% -> 0%
where the time goes in v2:
time: 87.5 us; the launch traced here: 87.4 us
  Pallas kernels  86 us (98%)
  between operations  1.45 us (2%)
    pallas_call x1, Pallas kernels, shards(): pl.pallas_call(kernel, out_shape=outs, in_specs=[hbm, hbm, hbm, hbm, pl.B...  84.2 us
    pallas_call x1, Pallas kernels, shards(): pl.pallas_call(hand_over, out_shape=outs, in_specs=[hbm, hbm], out_specs=...  1.76 us

profile of v2, /device:TPU:1, one launch (start us, length us, event | category | flops | bytes accessed | tf_op | source)
XLA Modules:
  0.0 87.4 jit_solution(7146635502019123621)
XLA Ops:
  1.3 84.2 %lobpcg_step.1 = (bf16[512,128]{1,0:T(8,128)(2,1)}, f32[256,256]{1,0:T(8,128)}) custom-call(bf16[512,128]{1,0:T(8,128)(2,1)} %refs_0_.1, bf16[384,128,128]{2,1,0:T(8,128)(2,1)} %bitcast.3, s32[1,384]{1,0:T(1,128)} %bitcast.4, s32[1,384]{1,0:T(1,128)} %bitcast.5, s32[1,1]{1,0:T(1,128)S(6)} %copy.7.refs_4_), custom_call_target="tpu_custom_call" | custom-call | tf_op jit(solution)/shard_map/lobpcg_step/pallas_call | solution.py:594
  85.5 1.8 %hand_over.1 = (bf16[512,128]{1,0:T(8,128)(2,1)}, f32[256,256]{1,0:T(8,128)}) custom-call(bf16[512,128]{1,0:T(8,128)(2,1)} %get-tuple-element.4.search_ref, f32[256,256]{1,0:T(8,128)} %get-tuple-element.5.projected_ref), custom_call_target="tpu_custom_call" | custom-call | tf_op jit(solution)/shard_map/hand_over/pallas_call | solution.py:635

commit v3 on v2

--- a/solution.py
+++ b/solution.py
@@ -86,66 +86,56 @@
     return ints, floats
 
 
-def factor_inverse(gram):
-    left = [gram[8 * i:8 * i + 8] for i in range(16)]
-    right = [flag(iota((8, BS), 1) == iota((8, BS), 0) + 8 * i) for i in range(16)]
+def half_inverse(block):
+    both = jnp.concatenate([block, flag(iota((HALF, HALF), 0) == iota((HALF, HALF), 1))], axis=1)
+    rows = [both[8 * i:8 * i + 8] for i in range(8)]
     sub = iota((8, BS), 0)
     out = []
 
     def wide(v):
         return jnp.broadcast_to(v, (8, BS))
 
-    for k in range(16):
+    for k in range(8):
         c = 8 * k
-        lanes = [wide(left[k][:, c + n:c + n + 1]) for n in range(8)]
+        lanes = [wide(rows[k][:, c + n:c + n + 1]) for n in range(8)]
         elem = [[wide(lanes[n][j:j + 1]) if n <= j else None for n in range(8)] for j in range(8)]
         inv = [[None] * 8 for unused in range(8)]
         roots, pivots = [], []
         for j in range(8):
             root = lax.rsqrt(elem[j][j])
             roots.append(root)
-            pivot = root * root
-            pivots.append(pivot)
-            mult = [elem[i][j] * pivot if i > j else None for i in range(8)]
+            pivots.append(root * root)
+            mult = [elem[i][j] * pivots[j] if i > j else None for i in range(8)]
             for i in range(j + 1, 8):
                 for n in range(j + 1, i + 1):
                     elem[i][n] = elem[i][n] - mult[i] * elem[n][j]
                 for n in range(j):
                     inv[i][n] = inv[i][n] - mult[i] * inv[j][n]
                 inv[i][j] = -mult[i]
-        lrows = [wide(left[k][j:j + 1]) for j in range(8)]
-        rrows = [wide(right[k][j:j + 1]) for j in range(8)]
-
-        def solved(rows):
-            first = []
-            for j in range(8):
-                total = rows[j]
-                for n in range(j):
-                    total = total + inv[j][n] * rows[n]
-                first.append(total)
+        held = [wide(rows[k][j:j + 1]) for j in range(8)]
+        first = []
+        for j in range(8):
+            total = held[j]
+            for n in range(j):
+                total = total + inv[j][n] * held[n]
+            first.append(total)
+        if k < 7:
             scaled = [first[j] * pivots[j] for j in range(8)]
-            second = []
+            solved = []
             for j in range(8):
                 total = scaled[j]
                 for n in range(j + 1, 8):
                     total = total + inv[n][j] * scaled[n]
-                second.append(total)
-            return first, second
-
-        unused, lsol = solved(lrows)
-        rfirst, rsol = solved(rrows)
-        for i in range(k + 1, 16):
-            for j in range(8):
-                f = wide(left[i][:, c + j:c + j + 1])
-                left[i] = left[i] - f * lsol[j]
-                right[i] = right[i] - f * rsol[j]
-        rows = jnp.zeros((8, BS), F32)
+                solved.append(total)
+            factors = [[wide(rows[i][:, c + j:c + j + 1]) for j in range(8)] for i in range(k + 1, 8)]
+            for i in range(k + 1, 8):
+                for j in range(8):
+                    rows[i] = rows[i] - factors[i - k - 1][j] * solved[j]
+        done = jnp.zeros((8, BS), F32)
         for j in range(8):
-            rows = jnp.where(sub == j, rfirst[j] * roots[j], rows)
-        out.append(rows)
-        if k in (3, 11):
-            yield None
-    yield jnp.concatenate(out, axis=0)
+            done = jnp.where(sub == j, first[j] * roots[j], done)
+        out.append(done)
+    return jnp.concatenate(out, axis=0)[:, HALF:]
 
 
 def step_kernel(inverse, x_hbm, w_hbm, row_hbm, col_hbm, cnt_ref, search_hbm, proj_hbm,
@@ -154,7 +144,7 @@
                 siba_s, siba_r, sibb_s, sibb_r, hi_s, hi_r, lo_s, lo_r, deg_s, deg_r,
                 lap_ref, deg_ref, x_group, l_group,
                 a_part, a_r1, a_b2, a_b3, a_res, b_part, b_r1, b_b2, b_res,
-                send_sem, recv_sem, local_sem):
+                fence_ref, send_sem, recv_sem, local_sem):
     slab1, slab2 = (slab1a, slab1b), (slab2a, slab2b)
     sib_s, sib_r = (siba_s, sibb_s), (siba_r, sibb_r)
     a = lax.axis_index("rows")
@@ -162,6 +152,15 @@
     y, z = a // NZ, a % NZ
     xx, core = b // 2, b % 2
     counter = [0]
+    never = jnp.where(a >= NY * NZ, 1, 0)
+
+    def fence():
+        def body(unused, carry):
+            fence_ref[...] = jnp.zeros_like(fence_ref)
+            return carry
+
+        lax.fori_loop(0, never, body, 0)
+
 
     def ydev(d):
         return {"rows": ((y + d + NY) % NY) * NZ + z, "cols": b}
@@ -230,9 +229,10 @@
         for h in range(2):
             slab1[h][p * 32 + (place[p][0] * 4 + place[p][1]) * 2 + t] = xt[h * HALF:(h + 1) * HALF]
     w_ref[SLOTS] = jnp.zeros((BS, BS), BF16)
+    fence()
     pl.semaphore_wait(barrier, len(partners))
 
-    def gather(slab):
+    def gather(slab, direct):
         def first(p, d):
             return ydev(d) if p == 0 else zdev(d)
 
@@ -258,6 +258,11 @@
             pair[1].wait_recv()
             two = half(p, (i + 1) % 4, j, 1)
             send(two, two, second(p, -1), k)
+
+        def spread_all(p, j):
+            ref = block(p, place[p][0], j)
+            for d in (2, 1, -1):
+                send(ref, ref, second(p, d), ends)
 
         near, own, side, far = [], [], [], []
         ends = new_sem()
@@ -269,6 +274,22 @@
             i, j = place[p]
             ref = block(p, i, j)
             far.append(send(ref, ref, first(p, 2)))
+        if direct:
+            for p in range(2):
+                spread_all(p, place[p][1])
+            yield
+            for p in range(2):
+                for n, j in enumerate((3, 1)):
+                    near[p][n].wait_recv()
+                    spread_all(p, (place[p][1] + j) % 4)
+            yield
+            for p in range(2):
+                far[p].wait_recv()
+                spread_all(p, (place[p][1] + 2) % 4)
+            yield
+            wait_bytes(slab.at[pl.ds(0, 48)], ends)
+            yield
+            return
         for p in range(2):
             own.append(spread(p, place[p][1]))
         yield
@@ -280,11 +301,8 @@
             side.append((one, spread(p, (j + 1) % 4)))
         yield
         for p in range(2):
-            i, j = place[p]
             far[p].wait_recv()
-            ref = block(p, i, (j + 2) % 4)
-            for d in (2, 1, -1):
-                send(ref, ref, second(p, d), ends)
+            spread_all(p, (place[p][1] + 2) % 4)
         yield
         for p in range(2):
             pass_on(p, place[p][1], own[p], ends)
@@ -306,8 +324,10 @@
         copy.wait_recv()
         yield
 
-    g1 = [gather(slab1[h]) for h in range(2)]
+    fence()
+    g1 = [gather(slab1[h], h == 1) for h in range(2)]
     next(g1[0])
+    fence()
     row_copy.wait()
     col_copy.wait()
     ints, floats = sort_slots(row_ref[...], col_ref[...], cnt_ref[0, 0], a)
@@ -325,22 +345,36 @@
         w_copies[n].wait()
         lax.fori_loop(n * PART, (n + 1) * PART, body, 0, unroll=16)
 
+    fence()
     flip(0)
+    fence()
     next(g1[0])
+    fence()
     next(g1[1])
+    fence()
     flip(1)
+    fence()
     next(g1[0])
+    fence()
     next(g1[0])
+    fence()
     flip(2)
+    fence()
     next(g1[0])
+    fence()
     next(g1[1])
+    fence()
     flip(3)
+    fence()
     next(g1[1])
-    next(g1[1])
+    xg = group_gather(x_group)
+    next(xg)
+    fence()
     ints_copy.wait()
     floats_copy.wait()
     xx_mat = sum(nt(xt_ref[r].astype(BF16), xt_ref[r].astype(BF16)) for r in range(4))
     a_part[:, 0] = xx_mat.reshape(8, 16, BS)
+    fence()
     next(g1[0])
 
     def pick(kind, at, top):
@@ -454,26 +488,34 @@
         wait_bytes(res.at[pl.ds(0, 7)], sems[3])
         yield
 
-    xg = group_gather(x_group)
+    fence()
+    product(slab1[0], 0, True, [])
+    fence()
+    reduce_start(0)
+    fence()
+    next(g1[1])
+
+    fence()
+    product(slab1[1], 1, False, [(1, lambda: reduce_middle(0))])
     next(xg)
-    product(slab1[0], 0, True, [(1, lambda: next(g1[1]))])
-    reduce_start(0)
-    next(g1[1])
-
-    def middle():
-        reduce_middle(0)
-        next(xg)
-
-    product(slab1[1], 1, False, [(2, middle)])
+    fence()
     reduce_start(1)
+    fence()
     reduce_end(0)
-    g2 = [gather(slab2[h]) for h in range(2)]
+    fence()
+    g2 = [gather(slab2[h], h == 1) for h in range(2)]
     next(g2[0])
+    fence()
     reduce_middle(1)
+    fence()
     next(g2[0])
+    fence()
     next(g2[0])
+    fence()
     reduce_end(1)
+    fence()
     next(g2[1])
+    fence()
     lap_all = joined(lap_ref)
     a_part[:, 1] = nt(joined(xt_ref), lap_all, HI).reshape(8, 16, BS)
     a_part[:, 2] = nt(lap_all, lap_all, HI).reshape(8, 16, BS)
@@ -481,30 +523,40 @@
     next(reduce_a)
     lg = group_gather(l_group)
     next(lg)
+    fence()
     next(g2[0])
+    fence()
     next(g2[0])
+    fence()
     scaled = joined(lap_ref) * jnp.concatenate([jnp.broadcast_to(deg_ref[r][:1], (BS, BS)) for r in range(4)], axis=1)
     pair_rows = jnp.concatenate([joined(xt_ref), joined(lap_ref)], axis=0)
     b_part[...] = nt(scaled, pair_rows, HI).reshape(8, 16, 2 * BS)
+    fence()
     next(g2[1])
+    fence()
     next(g2[1])
-    next(g2[1])
+    fence()
     next(reduce_a)
+    fence()
     next(g2[0])
 
     def early():
-        next(g2[1])
         for h in range(2):
             for d in (2, 1, 3):
                 lo_copy[h, d] = send(lo_s.at[h, d - 1], lo_r.at[h, d - 1], xdev(d))
 
-    product(slab2[0], 0, False, [(1, early), (3, lambda: next(reduce_a))])
+    fence()
+    product(slab2[0], 0, False, [(1, early)])
+    fence()
     next(lg)
+    fence()
     next(g2[1])
-    next(reduce_a)
-    product(slab2[1], 1, False, [])
+    fence()
+    product(slab2[1], 1, False, [(1, lambda: next(reduce_a))])
+    fence()
     next(lg)
     next(xg)
+    fence()
     total = jnp.zeros((BS, 2 * BS), F32)
     for c in range(2):
         for k in range(4):
@@ -516,20 +568,13 @@
                 low = jnp.concatenate([l_group[c, k, r], l_group[c, k, r + 1]], axis=1)
                 total = total + nt(part.astype(BF16), jnp.concatenate([top, low], axis=0))
     b_part[...] = b_part[...] - total.reshape(8, 16, 2 * BS)
+    fence()
     sems_b = [new_sem() for unused in range(3)]
     for d in range(1, NCOL):
         send(b_part.at[(b + d) % NCOL], b_r1.at[d - 1], coldev(d), sems_b[0])
+    fence()
     next(reduce_a)
-    def mat(m):
-        return a_res[:, m].reshape(BS, BS) * inverse
-
-    gx, theta, s_mat = mat(0), mat(1), mat(2)
-    m = 2.0 * theta - nn(gx, theta, HI)
-    m_t = m.T
-    cross = nn(m_t, theta, HI)
-    gram = s_mat - cross.T - cross + nn(m_t, nn(gx, m, HI), HI)
-    factor = factor_inverse(gram)
-    next(factor)
+    fence()
     wait_bytes(b_r1, sems_b[0])
     part = b_part[b]
     for d in range(1, NCOL):
@@ -537,7 +582,27 @@
     b_b2[a] = part
     for d in range(1, NY * NZ):
         send(b_b2.at[a], b_b2.at[a], yzdev(d), sems_b[1])
-    next(factor)
+    fence()
+    next(reduce_a)
+    fence()
+    def mat(m):
+        return a_res[:, m].reshape(BS, BS) * inverse
+
+    gx, theta, s_mat = mat(0), mat(1), mat(2)
+    m = 2.0 * theta - nn(gx, theta, HI)
+    m_t = m.T
+    cross = nn(m_t, theta, HI)
+    gram = s_mat - cross.T - cross + nn(m_t, nn(gx, m, HI), HI)
+    fence()
+    inv_a = half_inverse(gram[:HALF, :HALF])
+    side = nt(gram[HALF:, :HALF], inv_a, HI)
+    fence()
+    inv_c = half_inverse(gram[HALF:, HALF:] - nt(side, side, HI))
+    corner = nn(inv_c, nn(side, inv_a, HI), HI)
+    t_t = jnp.concatenate(
+        [jnp.concatenate([inv_a, jnp.zeros((HALF, HALF), F32)], axis=1), jnp.concatenate([-corner, inv_c], axis=1)],
+        axis=0)
+    fence()
     wait_bytes(b_b2.at[pl.ds(0, NY * NZ - 1)], sems_b[1])
     part = b_b2[0]
     for k in range(1, NY * NZ):
@@ -545,10 +610,11 @@
     b_res[b] = part
     for d in range(1, NCOL):
         send(b_res.at[b], b_res.at[b], coldev(d), sems_b[2])
-    t_t = next(factor)
+    fence()
     for h in range(2):
         for d in (1, 3, 2):
             lo_copy[h, d].wait_recv()
+    fence()
     mt_t = nt(t_t, m, HI)
     for r in range(4):
         low = [sum(lo_r[h, d, r].astype(F32) for d in range(3)) for h in range(2)]
@@ -562,7 +628,9 @@
     tail = jnp.concatenate([t_t, -mt_t], axis=1)
     proj_ref[:BS, :BS] = theta
     proj_ref[BS:, :BS] = nn(t_t, s_mat - cross, HI)
+    fence()
     wait_bytes(b_res.at[pl.ds(0, 7)], sems_b[2])
+    fence()
     spun = nn(t_t, b_res[...].reshape(BS, 2 * BS) * inverse, HI)
     xq = spun[:, :BS] - e1
     qq = nt(jnp.concatenate([spun[:, BS:] - e2, xq], axis=1), tail, HI)
@@ -571,6 +639,7 @@
     proj_copy = pltpu.make_async_copy(proj_ref, proj_hbm, local_sem.at[4])
     proj_copy.start()
     assert counter[0] <= N_SEM
+    fence()
     whole = w_ref.at[pl.ds(0, sent[0] // BLOCK_BYTES)]
     assert sent[0] % BLOCK_BYTES == 0
     remote(whole, whole, sibling, 0).wait_send()
@@ -612,7 +681,7 @@
             buf(2, 4, 4, BS, BS, dtype=BF16), buf(2, 4, 4, BS, BS, dtype=BF16),
             buf(8, 3, 16, BS), buf(7, 3, 16, BS), buf(4, 3, 16, BS), buf(4, 3, 16, BS), buf(8, 3, 16, BS),
             buf(8, 16, 2 * BS), buf(7, 16, 2 * BS), buf(16, 16, 2 * BS), buf(8, 16, 2 * BS),
-            pltpu.SemaphoreType.DMA((1,)), pltpu.SemaphoreType.DMA((N_SEM,)), pltpu.SemaphoreType.DMA((10,)),
+            buf(8, BS), pltpu.SemaphoreType.DMA((1,)), pltpu.SemaphoreType.DMA((N_SEM,)), pltpu.SemaphoreType.DMA((10,)),
         ],
         compiler_params=pltpu.CompilerParams(
             collective_id=0, has_side_effects=True, vmem_limit_bytes=60 * 1024 * 1024),

time: 87.5 us -> 78 us (0.89)
  Pallas kernels: 86 us -> 76.4 us
    pallas_call x1, Pallas kernels: 84.2 us -> 74.6 us  [shards(): pl.pallas_call(kernel, out_shape=outs, in_specs=[hbm, hbm, hbm, hbm, pl.B...]
where the time goes in v3:
time: 78 us; the launch traced here: 77.8 us
  Pallas kernels  76.4 us (98%)
  between operations  1.45 us (2%)
    pallas_call x1, Pallas kernels, shards(): pl.pallas_call(kernel, out_shape=outs, in_specs=[hbm, hbm, hbm, hbm, pl.B...  74.6 us
    pallas_call x1, Pallas kernels, shards(): pl.pallas_call(hand_over, out_shape=outs, in_specs=[hbm, hbm], out_specs=...  1.76 us

profile of v3, /device:TPU:1, one launch (start us, length us, event | category | flops | bytes accessed | tf_op | source)
XLA Modules:
  0.0 77.8 jit_solution(2588098652874937375)
XLA Ops:
  1.3 74.6 %lobpcg_step.1 = (bf16[512,128]{1,0:T(8,128)(2,1)}, f32[256,256]{1,0:T(8,128)}) custom-call(bf16[512,128]{1,0:T(8,128)(2,1)} %refs_0_.1, bf16[384,128,128]{2,1,0:T(8,128)(2,1)} %bitcast.3, s32[1,384]{1,0:T(1,128)} %bitcast.4, s32[1,384]{1,0:T(1,128)} %bitcast.5, s32[1,1]{1,0:T(1,128)S(6)} %copy.7.refs_4_), custom_call_target="tpu_custom_call" | custom-call | tf_op jit(solution)/shard_map/lobpcg_step/pallas_call | solution.py:663
  75.9 1.8 %hand_over.1 = (bf16[512,128]{1,0:T(8,128)(2,1)}, f32[256,256]{1,0:T(8,128)}) custom-call(bf16[512,128]{1,0:T(8,128)(2,1)} %get-tuple-element.4.search_ref, f32[256,256]{1,0:T(8,128)} %get-tuple-element.5.projected_ref), custom_call_target="tpu_custom_call" | custom-call | tf_op jit(solution)/shard_map/hand_over/pallas_call | solution.py:704

commit v4 on v3

--- a/solution.py
+++ b/solution.py
@@ -86,7 +86,7 @@
     return ints, floats
 
 
-def half_inverse(block):
+def half_inverse(block, midway=None):
     both = jnp.concatenate([block, flag(iota((HALF, HALF), 0) == iota((HALF, HALF), 1))], axis=1)
     rows = [both[8 * i:8 * i + 8] for i in range(8)]
     sub = iota((8, BS), 0)
@@ -135,6 +135,8 @@
         for j in range(8):
             done = jnp.where(sub == j, first[j] * roots[j], done)
         out.append(done)
+        if k == 3 and midway is not None:
+            midway()
     return jnp.concatenate(out, axis=0)[:, HALF:]
 
 
@@ -198,15 +200,15 @@
     def wait_bytes(like, k):
         remote(like, like, sibling, k).wait_recv()
 
+    x_copy = pltpu.make_async_copy(x_hbm, x_ref, local_sem.at[3])
+    x_copy.start()
     barrier = pltpu.get_barrier_semaphore()
     partners = [coldev(d) for d in range(1, NCOL)] + [yzdev(d) for d in range(1, NY * NZ)]
     for device in partners:
         pl.semaphore_signal(barrier, inc=1, device_id=device, device_id_type=pl.DeviceIdType.MESH)
 
-    x_copy = pltpu.make_async_copy(x_hbm, x_ref, local_sem.at[3])
     row_copy = pltpu.make_async_copy(row_hbm, row_ref, local_sem.at[4])
     col_copy = pltpu.make_async_copy(col_hbm, col_ref, local_sem.at[5])
-    x_copy.start()
     row_copy.start()
     col_copy.start()
     w_copies = [pltpu.make_async_copy(w_hbm.at[pl.ds(n * PART, PART)], w_ref.at[pl.ds(n * PART, PART)],
@@ -325,8 +327,11 @@
         yield
 
     fence()
-    g1 = [gather(slab1[h], h == 1) for h in range(2)]
+    g1 = [gather(slab1[h], False) for h in range(2)]
     next(g1[0])
+    next(g1[1])
+    xg = group_gather(x_group)
+    next(xg)
     fence()
     row_copy.wait()
     col_copy.wait()
@@ -350,24 +355,21 @@
     fence()
     next(g1[0])
     fence()
+    flip(1)
+    fence()
+    next(g1[0])
+    fence()
+    next(g1[0])
+    fence()
+    flip(2)
+    fence()
+    next(g1[0])
+    fence()
     next(g1[1])
     fence()
-    flip(1)
-    fence()
-    next(g1[0])
-    fence()
-    next(g1[0])
-    fence()
-    flip(2)
-    fence()
-    next(g1[0])
+    flip(3)
     fence()
     next(g1[1])
-    fence()
-    flip(3)
-    fence()
-    next(g1[1])
-    xg = group_gather(x_group)
     next(xg)
     fence()
     ints_copy.wait()
@@ -489,7 +491,7 @@
         yield
 
     fence()
-    product(slab1[0], 0, True, [])
+    product(slab1[0], 0, True, [(1, lambda: (next(g1[1]), next(g1[1])))])
     fence()
     reduce_start(0)
     fence()
@@ -497,16 +499,17 @@
 
     fence()
     product(slab1[1], 1, False, [(1, lambda: reduce_middle(0))])
-    next(xg)
     fence()
     reduce_start(1)
     fence()
     reduce_end(0)
     fence()
-    g2 = [gather(slab2[h], h == 1) for h in range(2)]
+    g2 = [gather(slab2[h], False) for h in range(2)]
     next(g2[0])
     fence()
     reduce_middle(1)
+    fence()
+    next(g2[0])
     fence()
     next(g2[0])
     fence()
@@ -526,21 +529,21 @@
     fence()
     next(g2[0])
     fence()
-    next(g2[0])
+    next(g2[1])
+    fence()
+    next(g2[1])
     fence()
     scaled = joined(lap_ref) * jnp.concatenate([jnp.broadcast_to(deg_ref[r][:1], (BS, BS)) for r in range(4)], axis=1)
     pair_rows = jnp.concatenate([joined(xt_ref), joined(lap_ref)], axis=0)
     b_part[...] = nt(scaled, pair_rows, HI).reshape(8, 16, 2 * BS)
     fence()
-    next(g2[1])
-    fence()
-    next(g2[1])
-    fence()
     next(reduce_a)
     fence()
     next(g2[0])
 
     def early():
+        next(g2[1])
+        next(g2[1])
         for h in range(2):
             for d in (2, 1, 3):
                 lo_copy[h, d] = send(lo_s.at[h, d - 1], lo_r.at[h, d - 1], xdev(d))
@@ -596,20 +599,23 @@
     fence()
     inv_a = half_inverse(gram[:HALF, :HALF])
     side = nt(gram[HALF:, :HALF], inv_a, HI)
-    fence()
-    inv_c = half_inverse(gram[HALF:, HALF:] - nt(side, side, HI))
+    def gathered():
+        fence()
+        wait_bytes(b_b2.at[pl.ds(0, NY * NZ - 1)], sems_b[1])
+        part = b_b2[0]
+        for k in range(1, NY * NZ):
+            part = part + b_b2[k]
+        b_res[b] = part
+        for d in range(1, NCOL):
+            send(b_res.at[b], b_res.at[b], coldev(d), sems_b[2])
+        fence()
+
+    fence()
+    inv_c = half_inverse(gram[HALF:, HALF:] - nt(side, side, HI), gathered)
     corner = nn(inv_c, nn(side, inv_a, HI), HI)
     t_t = jnp.concatenate(
         [jnp.concatenate([inv_a, jnp.zeros((HALF, HALF), F32)], axis=1), jnp.concatenate([-corner, inv_c], axis=1)],
         axis=0)
-    fence()
-    wait_bytes(b_b2.at[pl.ds(0, NY * NZ - 1)], sems_b[1])
-    part = b_b2[0]
-    for k in range(1, NY * NZ):
-        part = part + b_b2[k]
-    b_res[b] = part
-    for d in range(1, NCOL):
-        send(b_res.at[b], b_res.at[b], coldev(d), sems_b[2])
     fence()
     for h in range(2):
         for d in (1, 3, 2):

time: 78 us -> 76.4 us (0.979)
  Pallas kernels: 76.4 us -> 74.8 us
    pallas_call x1, Pallas kernels: 74.6 us -> 73 us  [shards(): pl.pallas_call(kernel, out_shape=outs, in_specs=[hbm, hbm, hbm, hbm, pl.B...]
where the time goes in v4:
time: 76.4 us; the launch traced here: 76.2 us
  Pallas kernels  74.8 us (98%)
  between operations  1.45 us (2%)
    pallas_call x1, Pallas kernels, shards(): pl.pallas_call(kernel, out_shape=outs, in_specs=[hbm, hbm, hbm, hbm, pl.B...  73 us
    pallas_call x1, Pallas kernels, shards(): pl.pallas_call(hand_over, out_shape=outs, in_specs=[hbm, hbm], out_specs=...  1.76 us

profile of v4, /device:TPU:1, one launch (start us, length us, event | category | flops | bytes accessed | tf_op | source)
XLA Modules:
  0.0 76.2 jit_solution(4630223507200156733)
XLA Ops:
  1.3 73.0 %lobpcg_step.1 = (bf16[512,128]{1,0:T(8,128)(2,1)}, f32[256,256]{1,0:T(8,128)}) custom-call(bf16[512,128]{1,0:T(8,128)(2,1)} %refs_0_.1, bf16[384,128,128]{2,1,0:T(8,128)(2,1)} %bitcast.3, s32[1,384]{1,0:T(1,128)} %bitcast.4, s32[1,384]{1,0:T(1,128)} %bitcast.5, s32[1,1]{1,0:T(1,128)S(6)} %copy.7.refs_4_), custom_call_target="tpu_custom_call" | custom-call | tf_op jit(solution)/shard_map/lobpcg_step/pallas_call | solution.py:669
  74.3 1.8 %hand_over.1 = (bf16[512,128]{1,0:T(8,128)(2,1)}, f32[256,256]{1,0:T(8,128)}) custom-call(bf16[512,128]{1,0:T(8,128)(2,1)} %get-tuple-element.4.search_ref, f32[256,256]{1,0:T(8,128)} %get-tuple-element.5.projected_ref), custom_call_target="tpu_custom_call" | custom-call | tf_op jit(solution)/shard_map/hand_over/pallas_call | solution.py:710

commit v5 on v4

--- a/solution.py
+++ b/solution.py
@@ -632,17 +632,19 @@
     e1 = nt(mt_t, theta, HI)
     e2 = nn(mt_t, s_mat, HI)
     tail = jnp.concatenate([t_t, -mt_t], axis=1)
-    proj_ref[:BS, :BS] = theta
-    proj_ref[BS:, :BS] = nn(t_t, s_mat - cross, HI)
+    proj_ref[0, :BS] = theta
+    proj_ref[0, BS:] = nn(t_t, s_mat - cross, HI)
+    left_copy = pltpu.make_async_copy(proj_ref.at[0], proj_hbm.at[:, pl.ds(0, BS)], local_sem.at[5])
+    left_copy.start()
     fence()
     wait_bytes(b_res.at[pl.ds(0, 7)], sems_b[2])
     fence()
     spun = nn(t_t, b_res[...].reshape(BS, 2 * BS) * inverse, HI)
     xq = spun[:, :BS] - e1
     qq = nt(jnp.concatenate([spun[:, BS:] - e2, xq], axis=1), tail, HI)
-    proj_ref[:BS, BS:] = xq.T
-    proj_ref[BS:, BS:] = qq.T
-    proj_copy = pltpu.make_async_copy(proj_ref, proj_hbm, local_sem.at[4])
+    proj_ref[1, :BS] = xq.T
+    proj_ref[1, BS:] = qq.T
+    proj_copy = pltpu.make_async_copy(proj_ref.at[1], proj_hbm.at[:, pl.ds(BS, BS)], local_sem.at[4])
     proj_copy.start()
     assert counter[0] <= N_SEM
     fence()
@@ -650,6 +652,7 @@
     assert sent[0] % BLOCK_BYTES == 0
     remote(whole, whole, sibling, 0).wait_send()
     search_copy.wait()
+    left_copy.wait()
     proj_copy.wait()
 
 
@@ -673,7 +676,7 @@
         out_specs=(hbm, hbm),
         scratch_shapes=[
             buf(4 * BS, BS, dtype=BF16), buf(1, SLOTS, dtype=jnp.int32), buf(1, SLOTS, dtype=jnp.int32),
-            buf(4 * BS, BS, dtype=BF16), buf(2 * BS, 2 * BS),
+            buf(4 * BS, BS, dtype=BF16), buf(2, 2 * BS, BS),
             buf(SLOTS + 1, BS, BS, dtype=BF16),
             buf(64, HALF, BS, dtype=BF16), buf(64, HALF, BS, dtype=BF16),
             buf(64, HALF, BS, dtype=BF16), buf(64, HALF, BS, dtype=BF16),
@@ -696,12 +699,15 @@
       block_count.reshape(1, 1))
 
     def hand_over(search_ref, projected_ref, search_out, projected_out, search_v, projected_v, sems):
-        pairs = [(search_ref, search_v, search_out), (projected_ref, projected_v, projected_out)]
+        pairs = [(search_ref, search_v, search_out)]
+        for n in range(2):
+            rows = pl.ds(n * BS, BS)
+            pairs.append((projected_ref.at[rows], projected_v.at[rows], projected_out.at[rows]))
         reads = [pltpu.make_async_copy(src, mid, sems.at[n]) for n, (src, mid, dst) in enumerate(pairs)]
-        writes = [pltpu.make_async_copy(mid, dst, sems.at[n + 2]) for n, (src, mid, dst) in enumerate(pairs)]
+        writes = [pltpu.make_async_copy(mid, dst, sems.at[n + 3]) for n, (src, mid, dst) in enumerate(pairs)]
         for copy in reads:
             copy.start()
-        for n in range(2):
+        for n in range(3):
             reads[n].wait()
             writes[n].start()
         for copy in writes:
@@ -709,7 +715,7 @@
 
     return pl.pallas_call(
         hand_over, out_shape=outs, in_specs=[hbm, hbm], out_specs=(hbm, hbm),
-        scratch_shapes=[buf(4 * BS, BS, dtype=BF16), buf(2 * BS, 2 * BS), pltpu.SemaphoreType.DMA((4,))],
+        scratch_shapes=[buf(4 * BS, BS, dtype=BF16), buf(2 * BS, 2 * BS), pltpu.SemaphoreType.DMA((6,))],
         name="hand_over",
     )(search, projected)
 

time: 76.4 us -> 76.3 us (level)
  no operation moved by 1% of the time
where the time goes in v5:
time: 76.3 us; the launch traced here: 76.2 us
  Pallas kernels  74.7 us (98%)
  between operations  1.45 us (2%)
    pallas_call x1, Pallas kernels, shards(): pl.pallas_call(kernel, out_shape=outs, in_specs=[hbm, hbm, hbm, hbm, pl.B...  73 us
    pallas_call x1, Pallas kernels, shards(): pl.pallas_call(hand_over, out_shape=outs, in_specs=[hbm, hbm], out_specs=...  1.74 us

profile of v5, /device:TPU:1, one launch (start us, length us, event | category | flops | bytes accessed | tf_op | source)
XLA Modules:
  0.0 76.2 jit_solution(14897061485674857510)
XLA Ops:
  1.3 73.0 %lobpcg_step.1 = (bf16[512,128]{1,0:T(8,128)(2,1)}, f32[256,256]{1,0:T(8,128)}) custom-call(bf16[512,128]{1,0:T(8,128)(2,1)} %refs_0_.1, bf16[384,128,128]{2,1,0:T(8,128)(2,1)} %bitcast.3, s32[1,384]{1,0:T(1,128)} %bitcast.4, s32[1,384]{1,0:T(1,128)} %bitcast.5, s32[1,1]{1,0:T(1,128)S(6)} %copy.7.refs_4_), custom_call_target="tpu_custom_call" | custom-call | tf_op jit(solution)/shard_map/lobpcg_step/pallas_call | solution.py:672
  74.3 1.7 %hand_over.1 = (bf16[512,128]{1,0:T(8,128)(2,1)}, f32[256,256]{1,0:T(8,128)}) custom-call(bf16[512,128]{1,0:T(8,128)(2,1)} %get-tuple-element.4.search_ref, f32[256,256]{1,0:T(8,128)} %get-tuple-element.5.projected_ref), custom_call_target="tpu_custom_call" | custom-call | tf_op jit(solution)/shard_map/hand_over/pallas_call | solution.py:716
